TPU v7x, 512 devices: a whole 4x4x16 slice. The times are simulated.
512 devices in a mesh: group: 16 (over z_lo, core), resp: 8 (over y, z_hi), vocab: 4 (over x).
Axes of the slice: x: 4, y: 4, z: 16 (z_hi: 2, z_lo: 8; z = z_hi * 8 + z_lo), core: 2. Of those that a mesh axis runs over, the one named last changes fastest.
Arguments:
- queries: bfloat16 [16, 32, 128, 5120], P('group', ('resp', 'vocab')), may hold values from -200 to 200
- own_kv: bfloat16 [16, 32, 128, 2, 640], P('group', ('resp', 'vocab')), may hold values from -6 to 6
- prefix_kv: bfloat16 [16, 128, 2, 640], P('group', ('resp', 'vocab')), may hold values from -20 to 20
- out_grad: bfloat16 [16, 32, 128, 5120], P('group', ('resp', 'vocab')), may hold values from -6 to 6
- lengths: int32 [16, 32], P('group', ('resp', 'vocab')), may hold values from 32 to 128
- advantages: float32 [16, 32], P('group', ('resp', 'vocab')), may hold values from -4 to 4
Outputs:
- query_grad: bfloat16 [16, 32, 128, 5120], P('group', ('resp', 'vocab'))
- own_kv_grad: bfloat16 [16, 32, 128, 2, 640], P('group', ('resp', 'vocab'))
- prefix_kv_grad: float32 [16, 128, 2, 640], P('group', ('resp', 'vocab'))
- token_scale: float32 [], replicated
All inputs are finite; a program needn't handle non-finite values.
Results may differ from a plain program's by a relative error of at most 0.039.
Values may be sent and summed in bfloat16 or wider, within the bound.
A program may use at most 64 MiB of HBM per device.

v0:
```python
import math

import jax
import jax.numpy as jnp
from jax import lax
from jax.sharding import PartitionSpec as P

DH = 128
KVH = 5
GQA = 8


def on_device(queries, own_kv, prefix_kv, out_grad, lengths, advantages):
    tokens_here = queries.shape[2]
    kv_width = own_kv.shape[4]
    factor = 1.0 / math.sqrt(DH)
    slots = tokens_here * lax.axis_size("group") * lax.axis_size("resp") * lax.axis_size("vocab")
    valid_total = lax.psum(lengths[0, 0], ("group", "resp", "vocab"))
    token_scale = jnp.float32(slots) / valid_total.astype(jnp.float32)
    gathered = lax.all_gather(prefix_kv, ("resp", "vocab"), axis=1, tiled=True)
    pre_keys = gathered[0, :, 0]
    pre_values = gathered[0, :, 1]
    own_keys = own_kv[0, 0, :, 0]
    own_values = own_kv[0, 0, :, 1]
    query_flat = queries[0, 0]
    positions = jnp.arange(tokens_here)
    causal = positions[:, None] >= positions[None, :]
    usable = (positions < lengths[0, 0]).astype(jnp.float32)
    row_weight = usable * advantages[0, 0] * token_scale
    grad_in = (out_grad[0, 0].astype(jnp.float32) * row_weight[:, None]).astype(jnp.bfloat16)
    width = GQA * DH
    query_parts, key_parts, value_parts, weight_parts, dscore_parts = ([], [], [], [], [])
    for head in range(KVH):
        head_query = query_flat[:, head * width : (head + 1) * width].reshape(tokens_here, GQA, DH)
        head_grad = grad_in[:, head * width : (head + 1) * width].reshape(tokens_here, GQA, DH)
        pre_key = pre_keys[:, head * DH : (head + 1) * DH]
        pre_value = pre_values[:, head * DH : (head + 1) * DH]
        own_key = own_keys[:, head * DH : (head + 1) * DH]
        own_value = own_values[:, head * DH : (head + 1) * DH]
        score_pre = (
            jnp.einsum("igd,jd->gij", head_query, pre_key, preferred_element_type=jnp.float32)
            * factor
        )
        score_own = (
            jnp.einsum("igd,jd->gij", head_query, own_key, preferred_element_type=jnp.float32)
            * factor
        )
        score_own = jnp.where(causal, score_own, -jnp.inf)
        row_peak = jnp.maximum(jnp.max(score_pre, axis=2), jnp.max(score_own, axis=2))
        exp_pre = jnp.exp(score_pre - row_peak[..., None])
        exp_own = jnp.exp(score_own - row_peak[..., None])
        row_total = jnp.sum(exp_pre, axis=2) + jnp.sum(exp_own, axis=2)
        prob_pre = exp_pre / row_total[..., None]
        prob_own = exp_own / row_total[..., None]
        weight_pre = prob_pre.astype(jnp.bfloat16)
        weight_own = prob_own.astype(jnp.bfloat16)
        mixed = jnp.einsum("gij,jd->igd", weight_pre, pre_value, preferred_element_type=jnp.float32)
        mixed = mixed + jnp.einsum(
            "gij,jd->igd", weight_own, own_value, preferred_element_type=jnp.float32
        )
        attended = mixed.astype(jnp.bfloat16)
        row_delta = jnp.einsum(
            "igd,igd->gi", head_grad, attended, preferred_element_type=jnp.float32
        )
        dprob_pre = jnp.einsum(
            "igd,jd->gij", head_grad, pre_value, preferred_element_type=jnp.float32
        )
        dprob_own = jnp.einsum(
            "igd,jd->gij", head_grad, own_value, preferred_element_type=jnp.float32
        )
        dscore_pre = (prob_pre * (dprob_pre - row_delta[..., None])).astype(jnp.bfloat16)
        dscore_own = (prob_own * (dprob_own - row_delta[..., None])).astype(jnp.bfloat16)
        head_qgrad = jnp.einsum(
            "gij,jd->igd", dscore_pre, pre_key, preferred_element_type=jnp.float32
        )
        head_qgrad = (
            head_qgrad
            + jnp.einsum("gij,jd->igd", dscore_own, own_key, preferred_element_type=jnp.float32)
        ) * factor
        query_parts.append(head_qgrad.reshape(tokens_here, width).astype(jnp.bfloat16))
        key_parts.append(
            jnp.einsum("gij,igd->jd", dscore_own, head_query, preferred_element_type=jnp.float32)
            * factor
        )
        value_parts.append(
            jnp.einsum("gij,igd->jd", weight_own, head_grad, preferred_element_type=jnp.float32)
        )
        weight_parts.append(weight_pre)
        dscore_parts.append(dscore_pre)
    query_grad = jnp.concatenate(query_parts, axis=1)
    own_grad = jnp.stack(
        [jnp.concatenate(key_parts, axis=1), jnp.concatenate(value_parts, axis=1)], axis=1
    ).astype(jnp.bfloat16)
    weight_all = jnp.stack(weight_parts, axis=0)
    dscore_all = jnp.stack(dscore_parts, axis=0)
    query_heads = query_flat.reshape(tokens_here, KVH, GQA, DH)
    grad_heads = grad_in.reshape(tokens_here, KVH, GQA, DH)
    shard_rows = prefix_kv.shape[1]
    grad_keys = (
        jnp.einsum("kgij,ikgd->jkd", dscore_all, query_heads, preferred_element_type=jnp.float32)
        * factor
    )
    grad_values = jnp.einsum(
        "kgij,ikgd->jkd", weight_all, grad_heads, preferred_element_type=jnp.float32
    )
    prefix_grad = lax.psum_scatter(
        jnp.stack(
            [
                grad_keys.reshape(shard_rows * lax.axis_size(("resp", "vocab")), kv_width),
                grad_values.reshape(shard_rows * lax.axis_size(("resp", "vocab")), kv_width),
            ],
            axis=1,
        ),
        ("resp", "vocab"),
        scatter_dimension=0,
        tiled=True,
    )
    return (query_grad[None, None], own_grad[None, None], prefix_grad[None], token_scale)


def solution(mesh):
    in_specs = (
        P("group", ("resp", "vocab"), None, None),
        P("group", ("resp", "vocab"), None, None, None),
        P("group", ("resp", "vocab"), None, None),
        P("group", ("resp", "vocab"), None, None),
        P("group", ("resp", "vocab")),
        P("group", ("resp", "vocab")),
    )
    out_specs = (
        P("group", ("resp", "vocab"), None, None),
        P("group", ("resp", "vocab"), None, None, None),
        P("group", ("resp", "vocab"), None, None),
        P(),
    )
    return jax.shard_map(
        on_device, mesh=mesh, in_specs=in_specs, out_specs=out_specs, check_vma=False
    )
```

profile of v0, /device:TPU:6, one launch (start us, length us, event | category | flops | bytes accessed | tf_op | source)
XLA Modules:
  0.0 878.1 jit_solution(14058199758747909417)
XLA Ops:
  7.2 2.4 fusion.162
  9.6 1.8 copy.153
  12.2 139.0 %all_gather.3 = bf16[1,128,2,640]{3,2,0,1:T(2,128)(2,1)S(1)} all-gather(bf16[1,4,2,640]{3,2,0,1:T(2,128)(2,1)S(1)} %bitcast.529), channel_id=1, replica_groups=mesh['group'=16,'resp'=8,'vocab'=4] {'resp','vocab'}, dimensions={1}, use_global_device_ids=true | all-gather | bytes 337920 | tf_op jit(solution)/shard_map/all_gather | solution.py:20
  154.5 1.1 fusion.135
  155.8 1.1 fusion.137
  157.2 1.1 fusion.139
  158.6 1.1 fusion.141
  160.1 1.1 fusion.143
  161.4 1.1 copy-done.58
  163.1 123.7 %psum.7 = s32[]{:T(128)} all-reduce(s32[]{:T(128)} %bitcast.20), channel_id=1, replica_groups=mesh['group'=16,'resp'=8,'vocab'=4] {'group','resp','vocab'}, use_global_device_ids=true, to_apply=%region_4.5 | all-reduce | flops 1 | bytes 8 | tf_op jit(solution)/shard_map/psum | solution.py:18
  288.2 1.4 copy.157
  289.7 1.7 fusion
  291.8 1.2 fusion.1
  293.0 1.9 copy.237
  294.9 1.7 copy.362
  296.5 1.1 fusion.161
  297.6 1.9 copy.322
  299.5 2.0 copy.304
  301.5 0.9 copy.286
  302.5 0.9 copy.268
  303.4 0.9 copy.250
  304.4 1.8 fusion.74
  311.2 0.9 bitcast_dynamic-update-slice_fusion.9
  312.2 1.0 bitcast_dynamic-update-slice_fusion.8
  313.3 1.0 bitcast_dynamic-update-slice_fusion.7
  314.4 1.0 bitcast_dynamic-update-slice_fusion.6
  315.5 1.0 bitcast_dynamic-update-slice_fusion.5
  317.5 1.4 pad_maximum_fusion
  330.7 1.2 copy.238
  332.6 1.3 dynamic-slice
  334.7 534.1 %all-reduce.3.cloned.1.call-done = f32[128,2,640]{2,1,0:T(2,128)} async-done(((f32[128,2,640]{2,1,0:T(2,128)}), f32[128,2,640]{2,1,0:T(2,128)}) %all-reduce.3.cloned.1.call-update) | async-done | bytes 655376
  868.8 1.3 dynamic-slice_bitcast_fusion
  (211 shorter events, 23.9 us)
Async XLA Ops:
  7.2 861.7 %all-reduce.3.cloned.1.call-start = ((), (), s32[]{:S(2)}) async-start(), calls=%async_computation | async-start | bytes 1310720
  9.6 144.1 %copy-start.31 = (bf16[1,1,128,1,640]{4,2,3,1,0:T(8,128)(2,1)}, bf16[1,1,128,1,640]{4,2,3,1,0:T(8,128)(2,1)S(1)}, u32[]{:S(2)}) copy-start(bf16[1,1,128,1,640]{4,2,3,1,0:T(8,128)(2,1)S(1)} %copy.363) | copy-start | bytes 491524
  11.6 140.4 %copy-start.15 = (bf16[128,1024]{0,1:T(8,128)(2,1)}, bf16[128,1024]{0,1:T(8,128)(2,1)S(1)}, u32[]{:S(2)}) copy-start(bf16[128,1024]{0,1:T(8,128)(2,1)S(1)} %get-tuple-element.30) | copy-start | bytes 786436
  11.6 140.9 %copy-start.13 = (bf16[128,1024]{0,1:T(8,128)(2,1)}, bf16[128,1024]{0,1:T(8,128)(2,1)S(1)}, u32[]{:S(2)}) copy-start(bf16[128,1024]{0,1:T(8,128)(2,1)S(1)} %get-tuple-element.29) | copy-start | bytes 786436
  11.6 141.4 %copy-start.11 = (bf16[128,1024]{0,1:T(8,128)(2,1)}, bf16[128,1024]{0,1:T(8,128)(2,1)S(1)}, u32[]{:S(2)}) copy-start(bf16[128,1024]{0,1:T(8,128)(2,1)S(1)} %get-tuple-element.28) | copy-start | bytes 786436
  11.6 141.8 %copy-start.9 = (bf16[128,1024]{0,1:T(8,128)(2,1)}, bf16[128,1024]{0,1:T(8,128)(2,1)S(1)}, u32[]{:S(2)}) copy-start(bf16[128,1024]{0,1:T(8,128)(2,1)S(1)} %get-tuple-element.27) | copy-start | bytes 786436
  151.7 2.2 copy-start.33
  151.7 8.3 copy-start.56
  152.2 2.0 copy-start.28
  152.5 3.1 copy-start.17
  152.7 4.2 copy-start.1
  153.0 4.1 copy-start.19
  153.2 5.1 copy-start.3
  153.5 5.0 copy-start.22
  153.7 6.0 copy-start.5
  154.0 5.9 copy-start.25
  154.2 7.0 copy-start.7
  160.1 128.1 %copy-start.36 = (bf16[1,1,128,5120]{3,2,1,0:T(8,128)(2,1)S(1)}, bf16[1,1,128,5120]{3,2,1,0:T(8,128)(2,1)}, u32[]{:S(2)}) copy-start(bf16[1,1,128,5120]{3,2,1,0:T(8,128)(2,1)} %param.9) | copy-start | bytes 3932164
  289.7 1.8 copy-start
  289.7 2.1 copy-start.59
  297.6 3.9 copy-start.39
  297.6 4.9 copy-start.41
  299.5 3.9 copy-start.43
  301.5 2.8 copy-start.26
  304.4 1.8 copy-start.23
  304.4 1.8 copy-start.48
  304.4 1.8 copy-start.54
  304.4 1.8 copy-start.65
  317.0 2.0 copy-start.42
  317.0 2.0 copy-start.55
  325.5 1.6 copy-start.12
  334.7 535.5 %copy-start.60 = (bf16[128,5120]{1,0:T(8,128)(2,1)}, bf16[128,5120]{1,0:T(8,128)(2,1)S(1)}, u32[]{:S(2)}) copy-start(bf16[128,5120]{1,0:T(8,128)(2,1)S(1)} %constant_dynamic-update-slice_fusion) | copy-start | bytes 3932164
  (35 other events, 38.0 us)
Sparse Core Ops, SparseCore 0:
  319.1 549.7 all-reduce.2
where the time goes:
time: 891 us; the launch traced here: 878 us
  waiting for transfers between devices  534 us (60%)
  blocking collectives  263 us (30%)
  local copies, waits for them, and re-layouts  33.4 us (4%)
  matrix products  24.2 us (3%)
  between operations  18.9 us (2%)
    unnamed x2, waiting for transfers between devices  534 us
    all_gather x1, blocking collectives, on_device(): gathered = lax.all_gather(prefix_kv, ('resp', 'vocab'), axis=1, tiled=True)  139 us
    psum x1, blocking collectives, on_device(): valid_total = lax.psum(lengths[0, 0], ('group', 'resp', 'vocab'))  124 us
    unnamed x147, local copies, waits for them, and re-layouts  25.2 us
  transfers between devices with their start and end apart: 1, of which 1 were waited for; matrix products, arithmetic and copies ran while one was open for 1% of the time, Pallas kernels for 0%

commit v1 on v0

v1 whole, which is shorter than its diff:
```python
import math

import jax
import jax.numpy as jnp
from jax import lax
from jax.experimental import pallas as pl
from jax.experimental.pallas import tpu as pltpu
from jax.sharding import PartitionSpec as P

DH = 128
KVH = 5
GQA = 8
TOKENS = 128
WIDTH = GQA * DH
PAIR = 2 * TOKENS
SIDE = 4
PLANE = SIDE * SIDE
FACTOR = 1.0 / math.sqrt(DH)
EXP_SCALE = FACTOR * math.log2(math.e)
LOW = -1e30
MESH = pl.DeviceIdType.MESH
F32 = jnp.float32
BF16 = jnp.bfloat16
LAST = (((1,), (1,)), ((), ()))


def dot_last(a, b):
    return lax.dot_general(a, b, LAST, preferred_element_type=F32)


def dot(a, b):
    return jnp.dot(a, b, preferred_element_type=F32)


def kernel(
    slots,
    len_ref, adv_ref, q_hbm, own_hbm, pre_hbm, do_hbm,
    qg_hbm, own_out, pre_out, scale_out,
    qs, dos, own, pre, own_k, own_v, pre_k, e_own, dp_own, stat, pt, dst, dqt, ogr, qg,
    z_out, z_in, gat, rs_out, rs_in, part, zs_out, zs_in, l_out, l_in,
    in_sem, small_sem, out_sem, z_sem, g_send, g_recv, rs_send, rs_recv, zs_send, zs_recv, l_send, l_recv,
):
    group = lax.axis_index("group")
    resp = lax.axis_index("resp")
    vocab = lax.axis_index("vocab")
    half = resp % 2
    row = resp // 2

    def mate(d, sign):
        there_y = (row + SIDE + sign * (d // SIDE)) % SIDE
        there_x = (vocab + SIDE + sign * (d % SIDE)) % SIDE
        return (group, there_y * 2 + half, there_x)

    opposite = (group, row * 2 + 1 - half, vocab)

    def other_group(stage):
        step = 2**stage
        bit = (group // step) % 2
        return (group + step - 2 * step * bit, resp, vocab)

    barrier = pltpu.get_barrier_semaphore()

    def greet(d, carry):
        pl.semaphore_signal(barrier, inc=1, device_id=mate(d, 1), device_id_type=MESH)
        return carry

    pl.semaphore_signal(barrier, inc=1, device_id=opposite, device_id_type=MESH)
    lax.fori_loop(1, PLANE, greet, 0)
    for stage in range(4):
        pl.semaphore_signal(barrier, inc=1, device_id=other_group(stage), device_id_type=MESH)

    pre_copy = pltpu.make_async_copy(pre_hbm, pre, small_sem.at[0])
    own_copy = pltpu.make_async_copy(own_hbm, own, small_sem.at[1])
    pre_copy.start()
    own_copy.start()

    def in_copies(k):
        cols = pl.ds(pl.multiple_of(k * WIDTH, WIDTH), WIDTH)
        return (
            pltpu.make_async_copy(q_hbm.at[:, cols], qs.at[k], in_sem.at[0, k]),
            pltpu.make_async_copy(do_hbm.at[:, cols], dos.at[k], in_sem.at[1, k]),
        )

    for k in range(KVH):
        for copy in in_copies(k):
            copy.start()

    tile_rows = lax.broadcasted_iota(jnp.int32, (16, DH), 0)
    length = len_ref[0, 0]
    z_out[0] = jnp.where(tile_rows // 4 == half, length.astype(F32), 0.0).astype(BF16)
    pre_copy.wait()
    shard = pre[...].astype(F32)
    blank = jnp.zeros((4, DH), F32)
    for k in range(KVH):
        cols = slice(k * DH, (k + 1) * DH)
        keys = shard[:, 0, cols]
        values = shard[:, 1, cols]
        low = jnp.concatenate([keys, blank, values, blank], axis=0)
        high = jnp.concatenate([blank, keys, blank, values], axis=0)
        z_out[k + 1] = jnp.where(half == 0, low, high).astype(BF16)

    pl.semaphore_wait(barrier, PLANE + 4)
    z_copy = pltpu.make_async_remote_copy(
        src_ref=z_out, dst_ref=z_in, send_sem=z_sem.at[0], recv_sem=z_sem.at[1],
        device_id=opposite, device_id_type=MESH,
    )
    z_copy.start()

    own_copy.wait()
    own_rows = own[...]
    own_keys = own_rows[:, 0, :]
    own_values = own_rows[:, 1, :]
    for k in range(KVH):
        own_k[k] = own_keys[:, k * DH : (k + 1) * DH]
        own_v[k] = own_values[:, k * DH : (k + 1) * DH]

    lane = lax.broadcasted_iota(jnp.int32, (1, PAIR), 1) % TOKENS
    weight = jnp.where(lane < length, adv_ref[0, 0], 0.0)
    key_at = lax.broadcasted_iota(jnp.int32, (TOKENS, PAIR), 0)
    query_at = lax.broadcasted_iota(jnp.int32, (TOKENS, PAIR), 1) % TOKENS
    causal = key_at <= query_at

    def pair_of(ref, k, c):
        return jnp.concatenate(
            [ref[k, :, (2 * c) * DH : (2 * c + 1) * DH], ref[k, :, (2 * c + 1) * DH : (2 * c + 2) * DH]], axis=0
        )

    def all_of(ref, k):
        return jnp.concatenate([ref[k, :, g * DH : (g + 1) * DH] for g in range(GQA)], axis=0)

    def own_part(k, carry):
        for copy in in_copies(k):
            copy.wait()
        keys = own_k[k]
        values = own_v[k]
        for c in range(GQA // 2):
            cols = slice(c * PAIR, (c + 1) * PAIR)
            score = jnp.where(causal, dot_last(keys, pair_of(qs, k, c)), LOW)
            peak = jnp.max(score, axis=0, keepdims=True)
            e = jnp.exp2((score - peak) * EXP_SCALE)
            dprob = dot_last(values, pair_of(dos, k, c))
            e_own[k, :, cols] = e
            dp_own[k, :, cols] = dprob
            stat[k, 0:1, cols] = peak
            stat[k, 1:2, cols] = jnp.sum(e, axis=0, keepdims=True)
            stat[k, 2:3, cols] = jnp.sum(e * dprob, axis=0, keepdims=True)
        return carry

    lax.fori_loop(0, 2, own_part, 0)

    z_copy.wait_recv()
    gat[0] = (z_out[...].astype(F32) + z_in[...].astype(F32)).astype(BF16)
    parts = ((0, 2), (2, 4))

    def spread(part_at):
        start, count = parts[part_at]

        def send(d, carry):
            pltpu.make_async_remote_copy(
                src_ref=gat.at[0, pl.ds(start, count)], dst_ref=gat.at[d, pl.ds(start, count)],
                send_sem=g_send.at[part_at], recv_sem=g_recv.at[part_at],
                device_id=mate(d, 1), device_id_type=MESH,
            ).start()
            return carry

        lax.fori_loop(1, PLANE, send, 0)

    def spread_all(part_at):
        start, count = parts[part_at]
        block = gat.at[pl.ds(1, PLANE - 1), pl.ds(start, count)]
        return pltpu.make_async_remote_copy(
            src_ref=block, dst_ref=block, send_sem=g_send.at[part_at], recv_sem=g_recv.at[part_at],
            device_id=opposite, device_id_type=MESH,
        )

    spread(0)
    spread(1)
    lax.fori_loop(2, KVH, own_part, 0)

    def length_copy(stage):
        return pltpu.make_async_remote_copy(
            src_ref=l_out.at[stage], dst_ref=l_in.at[stage], send_sem=l_send.at[stage], recv_sem=l_recv.at[stage],
            device_id=other_group(stage), device_id_type=MESH,
        )

    def length_step(stage):
        length_copy(stage).wait_recv()
        l_out[stage + 1] = l_out[stage] + l_in[stage]
        if stage < 3:
            length_copy(stage + 1).start()

    spread_all(0).wait_recv()
    counts = jnp.sum(gat[:, 0].astype(F32), axis=0)
    l_out[0] = jnp.broadcast_to(jnp.sum(counts, axis=0, keepdims=True) * 0.25, (8, DH))
    length_copy(0).start()

    def scatter(k):
        def send(d, carry):
            pltpu.make_async_remote_copy(
                src_ref=rs_out.at[k, d], dst_ref=rs_in.at[k, d], send_sem=rs_send.at[k], recv_sem=rs_recv.at[k],
                device_id=mate(d, -1), device_id_type=MESH,
            ).start()
            return carry

        lax.fori_loop(1, PLANE, send, 0)

    def scatter_all(k):
        return pltpu.make_async_remote_copy(
            src_ref=rs_out.at[k, pl.ds(1, PLANE - 1)], dst_ref=rs_in.at[k, pl.ds(1, PLANE - 1)],
            send_sem=rs_send.at[k], recv_sem=rs_recv.at[k], device_id=opposite, device_id_type=MESH,
        )

    def cross(k):
        return pltpu.make_async_remote_copy(
            src_ref=zs_out.at[k], dst_ref=zs_in.at[k], send_sem=zs_send.at[k], recv_sem=zs_recv.at[k],
            device_id=opposite, device_id_type=MESH,
        )

    def plane_sum(k):
        scatter_all(k).wait_recv()
        total = part[k] + jnp.sum(rs_in[k, 1:PLANE].astype(F32), axis=0)
        part[k] = total
        zs_out[k] = total.astype(BF16)
        cross(k).start()

    def prefix_part(k, carry):
        @pl.when(k == 1)
        def _():
            spread_all(1).wait_recv()

        tile = gat[:, k + 1].astype(F32)
        keys = tile[:, 0:8, :].reshape(TOKENS, DH).astype(BF16)
        values = tile[:, 8:16, :].reshape(TOKENS, DH).astype(BF16)
        pre_k[k] = keys
        for c in range(GQA // 2):
            cols = slice(c * PAIR, (c + 1) * PAIR)
            score = dot_last(keys, pair_of(qs, k, c))
            own_peak = stat[k, 0:1, cols]
            peak = jnp.maximum(own_peak, jnp.max(score, axis=0, keepdims=True))
            e = jnp.exp2((score - peak) * EXP_SCALE)
            dprob = dot_last(values, pair_of(dos, k, c))
            shrink = jnp.exp2((own_peak - peak) * EXP_SCALE)
            inverse = 1.0 / (jnp.sum(e, axis=0, keepdims=True) + shrink * stat[k, 1:2, cols])
            delta = (jnp.sum(e * dprob, axis=0, keepdims=True) + shrink * stat[k, 2:3, cols]) * inverse
            scaled = inverse * weight
            prob = e * scaled
            pt[:, cols] = prob.astype(BF16)
            dst[k, 0:TOKENS, cols] = (prob * (dprob - delta)).astype(BF16)
            stat[k, 3:4, cols] = shrink * scaled
            stat[k, 4:5, cols] = delta
        grad_k = dot(dst[k, 0:TOKENS, :], all_of(qs, k)) * FACTOR
        grad_v = dot(pt[...], all_of(dos, k))
        both = jnp.concatenate([grad_k.reshape(PLANE, 8, DH), grad_v.reshape(PLANE, 8, DH)], axis=1)
        part[k] = both[0]
        rs_out[k] = both.astype(BF16)
        scatter(k)

        @pl.when(k >= 2)
        def _():
            plane_sum(k - 2)

        @pl.when(k == 2)
        def _():
            length_step(0)

        return carry

    lax.fori_loop(0, KVH, prefix_part, 0)
    length_step(1)

    def own_grads(k):
        for c in range(GQA // 2):
            cols = slice(c * PAIR, (c + 1) * PAIR)
            prob = e_own[k, :, cols] * stat[k, 3:4, cols]
            pt[:, cols] = prob.astype(BF16)
            dst[k, TOKENS:PAIR, cols] = (prob * (dp_own[k, :, cols] - stat[k, 4:5, cols])).astype(BF16)
        ogr[k, 0] = dot(dst[k, TOKENS:PAIR, :], all_of(qs, k)) * FACTOR
        ogr[k, 1] = dot(pt[...], all_of(dos, k))
        keys = jnp.concatenate([pre_k[k].astype(F32).T, own_k[k].astype(F32).T], axis=1).astype(BF16)
        dqt[k] = dot(keys, dst[k]) * FACTOR

    def first_heads(k, carry):
        own_grads(k)
        plane_sum(k + 3)
        return carry

    def last_heads(k, carry):
        own_grads(k)
        return carry

    lax.fori_loop(0, 2, first_heads, 0)
    length_step(2)
    lax.fori_loop(2, KVH, last_heads, 0)
    length_step(3)
    scale = slots / l_out[4]
    scale_out[...] = scale[0:1, 0:1]
    one = scale[0:1, :]

    def out_copy(k):
        cols = pl.ds(pl.multiple_of(k * WIDTH, WIDTH), WIDTH)
        return pltpu.make_async_copy(qg.at[k], qg_hbm.at[:, cols], out_sem.at[k])

    def finish(k, carry):
        for g in range(GQA):
            cols = slice(g * DH, (g + 1) * DH)
            qg[k, :, cols] = (dqt[k, :, cols].T * one).astype(BF16)
        out_copy(k).start()
        return carry

    lax.fori_loop(0, KVH, finish, 0)
    for k in range(KVH):
        cols = slice(k * DH, (k + 1) * DH)
        own_out[0, :, cols] = (ogr[k, 0] * one).astype(BF16)
        own_out[1, :, cols] = (ogr[k, 1] * one).astype(BF16)

    for k in range(KVH):
        cols = slice(k * DH, (k + 1) * DH)
        cross(k).wait_recv()
        total = (part[k] + zs_in[k].astype(F32)) * one
        pre_out[:, 0, cols] = jnp.where(half == 0, total[0:4], total[4:8])
        pre_out[:, 1, cols] = jnp.where(half == 0, total[8:12], total[12:16])

    for k in range(KVH):
        out_copy(k).wait()
        scatter_all(k).wait_send()
        cross(k).wait_send()
    for stage in range(4):
        length_copy(stage).wait_send()
    spread_all(0).wait_send()
    spread_all(1).wait_send()
    z_copy.wait_send()


def on_device(queries, own_kv, prefix_kv, out_grad, lengths, advantages):
    slots = float(
        queries.shape[2] * lax.axis_size("group") * lax.axis_size("resp") * lax.axis_size("vocab")
    )
    width = KVH * WIDTH
    vmem = pltpu.VMEM
    dma = pltpu.SemaphoreType.DMA
    anywhere = pl.BlockSpec(memory_space=pl.ANY)
    in_smem = pl.BlockSpec(memory_space=pltpu.SMEM)
    in_vmem = pl.BlockSpec(memory_space=pltpu.VMEM)

    def body(*refs):
        kernel(slots, *refs)

    query_grad, own_grad, prefix_grad, token_scale = pl.pallas_call(
        body,
        out_shape=(
            jax.ShapeDtypeStruct((TOKENS, width), BF16),
            jax.ShapeDtypeStruct((2, TOKENS, KVH * DH), BF16),
            jax.ShapeDtypeStruct((4, 2, KVH * DH), F32),
            jax.ShapeDtypeStruct((1, 1), F32),
        ),
        in_specs=[in_smem, in_smem, anywhere, anywhere, anywhere, anywhere],
        out_specs=(anywhere, in_vmem, in_vmem, in_vmem),
        scratch_shapes=[
            vmem((KVH, TOKENS, WIDTH), BF16),
            vmem((KVH, TOKENS, WIDTH), BF16),
            vmem((TOKENS, 2, KVH * DH), BF16),
            vmem((4, 2, KVH * DH), BF16),
            vmem((KVH, TOKENS, DH), BF16),
            vmem((KVH, TOKENS, DH), BF16),
            vmem((KVH, TOKENS, DH), BF16),
            vmem((KVH, TOKENS, WIDTH), F32),
            vmem((KVH, TOKENS, WIDTH), F32),
            vmem((KVH, 8, WIDTH), F32),
            vmem((TOKENS, WIDTH), BF16),
            vmem((KVH, PAIR, WIDTH), BF16),
            vmem((KVH, DH, WIDTH), F32),
            vmem((KVH, 2, TOKENS, DH), F32),
            vmem((KVH, TOKENS, WIDTH), BF16),
            vmem((KVH + 1, 16, DH), BF16),
            vmem((KVH + 1, 16, DH), BF16),
            vmem((PLANE, KVH + 1, 16, DH), BF16),
            vmem((KVH, PLANE, 16, DH), BF16),
            vmem((KVH, PLANE, 16, DH), BF16),
            vmem((KVH, 16, DH), F32),
            vmem((KVH, 16, DH), BF16),
            vmem((KVH, 16, DH), BF16),
            vmem((5, 8, DH), F32),
            vmem((4, 8, DH), F32),
            dma((2, KVH)),
            dma((2,)),
            dma((KVH,)),
            dma((2,)),
            dma((2,)),
            dma((2,)),
            dma((KVH,)),
            dma((KVH,)),
            dma((KVH,)),
            dma((KVH,)),
            dma((4,)),
            dma((4,)),
        ],
        compiler_params=pltpu.CompilerParams(
            collective_id=0, has_side_effects=True, vmem_limit_bytes=48 * 1024 * 1024
        ),
        cost_estimate=pl.CostEstimate(
            flops=5 * KVH * 2 * WIDTH * PAIR * DH,
            bytes_accessed=5 * 1024 * 1024,
            transcendentals=KVH * WIDTH * PAIR,
        ),
    )(lengths, advantages, queries[0, 0], own_kv[0, 0], prefix_kv[0], out_grad[0, 0])
    own_grad = jnp.swapaxes(own_grad, 0, 1)
    return query_grad[None, None], own_grad[None, None], prefix_grad[None], token_scale[0, 0]


def solution(mesh):
    in_specs = (
        P("group", ("resp", "vocab"), None, None),
        P("group", ("resp", "vocab"), None, None, None),
        P("group", ("resp", "vocab"), None, None),
        P("group", ("resp", "vocab"), None, None),
        P("group", ("resp", "vocab")),
        P("group", ("resp", "vocab")),
    )
    out_specs = (
        P("group", ("resp", "vocab"), None, None),
        P("group", ("resp", "vocab"), None, None, None),
        P("group", ("resp", "vocab"), None, None),
        P(),
    )
    return jax.shard_map(
        on_device, mesh=mesh, in_specs=in_specs, out_specs=out_specs, check_vma=False
    )
```

time: 891 us -> 60 us (0.07); the launches traced: 878 us -> 59.1 us
  waiting for transfers between devices: 534 us -> 0 us
  blocking collectives: 263 us -> 0 us
  Pallas kernels: 0 us -> 48.4 us
  local copies, waits for them, and re-layouts: 33.4 us -> 7.02 us
  matrix products: 24.2 us -> 0 us
  between operations: 18.9 us -> 3.69 us
    unnamed x2 -> x0, waiting for transfers between devices: 534 us -> none
    all_gather x1 -> x0, blocking collectives: 139 us -> none  [on_device(): gathered = lax.all_gather(prefix_kv, ('resp', 'vocab'), axis=1, tiled=True)]
    psum x1 -> x0, blocking collectives: 124 us -> none  [on_device(): valid_total = lax.psum(lengths[0, 0], ('group', 'resp', 'vocab'))]
    pallas_call x0 -> x1, Pallas kernels: none -> 48.4 us  [on_device(): pl.pallas_call(body, out_shape=(jax.ShapeDtypeStruct((TOKENS, width), BF1...]
    dot_general x52 -> x0, matrix products: 24.2 us -> none  [the longest x5 5.45 us: on_device(): jnp.einsum('gij,jd->igd', weight_pre, pre_value, preferred_element_type=j...]
    unnamed x147 -> x11, local copies, waits for them, and re-layouts: 25.2 us -> 7.02 us
  transfers between devices with their start and end apart: 1 -> 0, of which waited for: 1 -> 0; matrix products, arithmetic and copies ran while one was open for 1% -> 0% of each run, Pallas kernels for 0% -> 0%
where the time goes in v1:
time: 60 us; the launch traced here: 59.1 us
  Pallas kernels  48.4 us (81%)
  local copies, waits for them, and re-layouts  7.02 us (12%)
  between operations  3.69 us (6%)
    pallas_call x1, Pallas kernels, on_device(): pl.pallas_call(body, out_shape=(jax.ShapeDtypeStruct((TOKENS, width), BF1...  48.4 us
    unnamed x11, local copies, waits for them, and re-layouts  7.02 us

profile of v1, /device:TPU:6, one launch (start us, length us, event | category | flops | bytes accessed | tf_op | source)
XLA Modules:
  0.0 59.1 jit_solution(10913344425922552835)
XLA Ops:
  1.9 0.0 copy-start
  1.9 1.3 %copy-done = bf16[1,1,128,5120]{3,2,1,0:T(8,128)(2,1)S(1)} copy-done((bf16[1,1,128,5120]{3,2,1,0:T(8,128)(2,1)S(1)}, bf16[1,1,128,5120]{3,2,1,0:T(8,128)(2,1)}, u32[]{:S(2)}) %copy-start) | copy-done | bytes 1310744
  3.2 0.0 copy-start.1
  3.2 1.3 %copy-done.1 = bf16[1,1,128,5120]{3,2,1,0:T(8,128)(2,1)S(1)} copy-done((bf16[1,1,128,5120]{3,2,1,0:T(8,128)(2,1)S(1)}, bf16[1,1,128,5120]{3,2,1,0:T(8,128)(2,1)}, u32[]{:S(2)}) %copy-start.1) | copy-done | bytes 1310744
  4.6 0.0 copy-start.2
  4.6 1.0 %copy-done.2 = bf16[1,1,128,2,640]{4,3,2,1,0:T(2,128)(2,1)S(1)} copy-done((bf16[1,1,128,2,640]{4,3,2,1,0:T(2,128)(2,1)S(1)}, bf16[1,1,128,2,640]{4,3,2,1,0:T(2,128)(2,1)}, u32[]{:S(2)}) %copy-start.2) | copy-done | bytes 327704
  5.5 0.0 copy-start.3
  5.5 0.7 %copy-done.3 = bf16[1,4,2,640]{3,2,1,0:T(2,128)(2,1)S(1)} copy-done((bf16[1,4,2,640]{3,2,1,0:T(2,128)(2,1)S(1)}, bf16[1,4,2,640]{3,2,1,0:T(2,128)(2,1)}, u32[]{:S(2)}) %copy-start.3) | copy-done | bytes 10264
  6.2 48.4 %shard_map.93 = (bf16[128,5120]{1,0:T(8,128)(2,1)S(1)}, bf16[2,128,640]{2,1,0:T(8,128)(2,1)S(1)}, f32[4,2,640]{2,1,0:T(2,128)S(1)}, f32[1,1]{1,0:T(1,128)}) custom-call(s32[1,1]{1,0:T(1,128)S(6)} %copy.14.refs_0_, f32[1,1]{1,0:T(1,128)S(6)} %copy.15.refs_1_, bf16[128,5120]{1,0:T(8,128)(2,1)S(1)} %bitcast.13, bf16[128,2,640]{2,1,0:T(2,128)(2,1)S(1)} %bitcast.15, ...), custom_call_target="tpu_custom_call" | custom-call | flops 1677721600 | bytes 5242880 | tf_op jit(solution)/shard_map/pallas_call | solution.py:348
  54.7 1.1 %copy.10 = bf16[1,1,128,2,640]{4,3,2,1,0:T(2,128)(2,1)} copy(bf16[1,1,128,2,640]{4,2,3,1,0:T(8,128)(2,1)S(1)} %bitcast.11) | data formatting | bytes 655360
  55.7 1.1 %copy.16 = bf16[1,1,128,5120]{3,2,1,0:T(8,128)(2,1)} copy(bf16[1,1,128,5120]{3,2,1,0:T(8,128)(2,1)S(1)} %bitcast.10) | data formatting | bytes 2621440
  56.8 0.6 %copy.17 = f32[1,4,2,640]{3,2,1,0:T(2,128)} copy(f32[1,4,2,640]{3,2,1,0:T(2,128)S(1)} %bitcast.12) | data formatting | bytes 40960
Async XLA Ops:
  1.9 1.3 %copy-start = (bf16[1,1,128,5120]{3,2,1,0:T(8,128)(2,1)S(1)}, bf16[1,1,128,5120]{3,2,1,0:T(8,128)(2,1)}, u32[]{:S(2)}) copy-start(bf16[1,1,128,5120]{3,2,1,0:T(8,128)(2,1)} %param.6) | copy-start | bytes 3932164
  3.2 1.3 %copy-start.1 = (bf16[1,1,128,5120]{3,2,1,0:T(8,128)(2,1)S(1)}, bf16[1,1,128,5120]{3,2,1,0:T(8,128)(2,1)}, u32[]{:S(2)}) copy-start(bf16[1,1,128,5120]{3,2,1,0:T(8,128)(2,1)} %param.9) | copy-start | bytes 3932164
  4.6 1.0 %copy-start.2 = (bf16[1,1,128,2,640]{4,3,2,1,0:T(2,128)(2,1)S(1)}, bf16[1,1,128,2,640]{4,3,2,1,0:T(2,128)(2,1)}, u32[]{:S(2)}) copy-start(bf16[1,1,128,2,640]{4,3,2,1,0:T(2,128)(2,1)} %param.7) | copy-start | bytes 983044
  5.5 0.7 %copy-start.3 = (bf16[1,4,2,640]{3,2,1,0:T(2,128)(2,1)S(1)}, bf16[1,4,2,640]{3,2,1,0:T(2,128)(2,1)}, u32[]{:S(2)}) copy-start(bf16[1,4,2,640]{3,2,1,0:T(2,128)(2,1)} %param.8) | copy-start | bytes 30724

commit v2 on v1

v2 whole, which is shorter than its diff:
```python
import math

import jax
import jax.numpy as jnp
from jax import lax
from jax.experimental import pallas as pl
from jax.experimental.pallas import tpu as pltpu
from jax.sharding import PartitionSpec as P

DH = 128
KVH = 5
GQA = 8
TOKENS = 128
WIDTH = GQA * DH
PAIR = 2 * TOKENS
SIDE = 4
PLANE = SIDE * SIDE
FACTOR = 1.0 / math.sqrt(DH)
EXP_SCALE = FACTOR * math.log2(math.e)
LOW = -1e30
MESH = pl.DeviceIdType.MESH
F32 = jnp.float32
BF16 = jnp.bfloat16
LAST = (((1,), (1,)), ((), ()))


def dot_last(a, b):
    return lax.dot_general(a, b, LAST, preferred_element_type=F32)


def dot(a, b):
    return jnp.dot(a, b, preferred_element_type=F32)


def kernel(
    slots,
    len_ref, adv_ref, q_hbm, own_hbm, pre_hbm, do_hbm,
    qg, own_out, pre_out, scale_out,
    qs, dos, own, pre, own_k, own_v, pre_k, e_own, dp_own, stat, pt, dst, ogr, own_t,
    z_out, z_in, gat, rs_out, rs_in, part, zs_out, zs_in, l_out, la_in, lb_in, lp_in, lz_in,
    in_sem, small_sem, z_send, z_recv, g_send, g_recv, rs_send, rs_recv, zs_send, zs_recv, l_send, l_recv,
):
    group = lax.axis_index("group")
    resp = lax.axis_index("resp")
    vocab = lax.axis_index("vocab")
    half = resp % 2
    row = resp // 2

    ahead, behind = [None], [None]
    for d in range(1, PLANE):
        down, over = d // SIDE, d % SIDE
        ahead.append((group, ((row + down) % SIDE) * 2 + half, (vocab + over) % SIDE))
        behind.append((group, ((row + SIDE - down) % SIDE) * 2 + half, (vocab + SIDE - over) % SIDE))
    opposite = (group, row * 2 + 1 - half, vocab)
    near = [None] + [((group // 4) * 4 + (group + o) % 4, resp, vocab) for o in range(1, 4)]
    far = [None] + [((group + 4 * o) % 16, resp, vocab) for o in range(1, 4)]

    barrier = pltpu.get_barrier_semaphore()
    partners = [opposite] + ahead[1:] + near[1:] + far[1:]
    for partner in partners:
        pl.semaphore_signal(barrier, inc=1, device_id=partner, device_id_type=MESH)

    pre_copy = pltpu.make_async_copy(pre_hbm, pre, small_sem.at[0])
    own_copy = pltpu.make_async_copy(own_hbm, own, small_sem.at[1])
    pre_copy.start()
    own_copy.start()

    def in_copies(k):
        cols = pl.ds(pl.multiple_of(k * WIDTH, WIDTH), WIDTH)
        return (
            pltpu.make_async_copy(q_hbm.at[:, cols], qs.at[k], in_sem.at[0, k]),
            pltpu.make_async_copy(do_hbm.at[:, cols], dos.at[k], in_sem.at[1, k]),
        )

    for k in range(KVH):
        for copy in in_copies(k):
            copy.start()

    length = len_ref[0, 0]
    l_out[0] = jnp.full((8, DH), length.astype(F32))
    blank = jnp.zeros((8, DH), F32)
    pre_copy.wait()
    shard = pre[...].astype(F32)
    mine = []
    for k in range(KVH):
        cols = slice(k * DH, (k + 1) * DH)
        mine.append(jnp.concatenate([shard[:, 0, cols], shard[:, 1, cols]], axis=0))
    for t in range(3):
        low = mine[2 * t]
        high = mine[2 * t + 1] if 2 * t + 1 < KVH else blank
        z_out[t] = jnp.concatenate([low, high], axis=0).astype(BF16)

    def z_copy(at):
        tiles = pl.ds(0, 1) if at == 0 else pl.ds(1, 2)
        return pltpu.make_async_remote_copy(
            src_ref=z_out.at[tiles], dst_ref=z_in.at[tiles], send_sem=z_send.at[at], recv_sem=z_recv.at[at],
            device_id=opposite, device_id_type=MESH,
        )

    def send(src, dst, sems, at, to):
        pltpu.make_async_remote_copy(
            src_ref=src, dst_ref=dst, send_sem=sems[0].at[at], recv_sem=sems[1].at[at],
            device_id=to, device_id_type=MESH,
        ).start()

    def landed(block, sems, at):
        return pltpu.make_async_remote_copy(
            src_ref=block, dst_ref=block, send_sem=sems[0].at[at], recv_sem=sems[1].at[at],
            device_id=opposite, device_id_type=MESH,
        )

    g_sems, l_sems, rs_sems = (g_send, g_recv), (l_send, l_recv), (rs_send, rs_recv)

    pl.semaphore_wait(barrier, len(partners))
    z_copy(0).start()
    z_copy(1).start()
    for o in range(1, 4):
        send(l_out.at[0], la_in.at[o], l_sems, 0, near[o])

    own_copy.wait()
    own_rows = own[...]
    own_keys = own_rows[:, 0, :]
    own_values = own_rows[:, 1, :]
    for k in range(KVH):
        own_k[k] = own_keys[:, k * DH : (k + 1) * DH]
        own_v[k] = own_values[:, k * DH : (k + 1) * DH]

    lane = lax.broadcasted_iota(jnp.int32, (1, PAIR), 1) % TOKENS
    weight = jnp.where(lane < length, adv_ref[0, 0], 0.0)
    key_at = lax.broadcasted_iota(jnp.int32, (TOKENS, PAIR), 0)
    query_at = lax.broadcasted_iota(jnp.int32, (TOKENS, PAIR), 1) % TOKENS
    causal = key_at <= query_at

    def pair_of(ref, k, c):
        return jnp.concatenate(
            [ref[k, :, (2 * c) * DH : (2 * c + 1) * DH], ref[k, :, (2 * c + 1) * DH : (2 * c + 2) * DH]], axis=0
        )

    def all_of(ref, k):
        return jnp.concatenate([ref[k, :, g * DH : (g + 1) * DH] for g in range(GQA)], axis=0)

    def own_part(k):
        for copy in in_copies(k):
            copy.wait()
        keys = own_k[k]
        values = own_v[k]
        for c in range(GQA // 2):
            cols = slice(c * PAIR, (c + 1) * PAIR)
            score = jnp.where(causal, dot_last(keys, pair_of(qs, k, c)), LOW)
            peak = jnp.max(score, axis=0, keepdims=True)
            e = jnp.exp2((score - peak) * EXP_SCALE)
            dprob = dot_last(values, pair_of(dos, k, c))
            e_own[k, :, cols] = e
            dp_own[k, :, cols] = dprob
            stat[k, 0:1, cols] = peak
            stat[k, 1:2, cols] = jnp.sum(e, axis=0, keepdims=True)
            stat[k, 2:3, cols] = jnp.sum(e * dprob, axis=0, keepdims=True)

    def own_parts(start, stop):
        def step(k, carry):
            own_part(k)
            return carry

        lax.fori_loop(start, stop, step, 0)

    def unit(k):
        at, rows = k // 2, slice(8 * (k % 2), 8 * (k % 2) + 8)
        here = z_out[at].astype(F32)[rows]
        there = z_in[at].astype(F32)[rows]
        first = jnp.where(half == 0, here, there)
        second = jnp.where(half == 0, there, here)
        gat[0, k] = jnp.concatenate([first[0:4], second[0:4], first[4:8], second[4:8]], axis=0).astype(BF16)

    parts = ((0, 1), (1, 1), (2, 3))

    def spread(at):
        start, count = parts[at]
        for d in range(1, PLANE):
            send(gat.at[0, pl.ds(start, count)], gat.at[d, pl.ds(start, count)], g_sems, at, ahead[d])

    def spread_all(at):
        start, count = parts[at]
        return landed(gat.at[pl.ds(1, PLANE - 1), pl.ds(start, count)], g_sems, at)

    own_part(0)
    landed(la_in.at[pl.ds(1, 3)], l_sems, 0).wait_recv()
    l_out[1] = l_out[0] + la_in[1] + la_in[2] + la_in[3]
    for o in range(1, 4):
        send(l_out.at[1], lb_in.at[o], l_sems, 1, far[o])
    own_parts(1, 3)
    z_copy(0).wait_recv()
    unit(0)
    spread(0)
    unit(1)
    spread(1)
    z_copy(1).wait_recv()
    for k in range(2, KVH):
        unit(k)
    spread(2)
    landed(lb_in.at[pl.ds(1, 3)], l_sems, 1).wait_recv()
    l_out[2] = l_out[1] + lb_in[1] + lb_in[2] + lb_in[3]
    for d in range(1, PLANE):
        send(l_out.at[2], lp_in.at[d], l_sems, 2, ahead[d])
    own_parts(3, KVH)

    def scatter_all(k):
        return landed(rs_out.at[k, pl.ds(1, PLANE - 1)], rs_sems, k)

    def cross(k):
        return pltpu.make_async_remote_copy(
            src_ref=zs_out.at[k], dst_ref=zs_in.at[k], send_sem=zs_send.at[k], recv_sem=zs_recv.at[k],
            device_id=opposite, device_id_type=MESH,
        )

    def plane_sum(k):
        landed(rs_in.at[k, pl.ds(1, PLANE - 1)], rs_sems, k).wait_recv()
        total = part[k] + jnp.sum(rs_in[k, 1:PLANE].astype(F32), axis=0)
        part[k] = total
        zs_out[k] = total.astype(BF16)
        cross(k).start()

    length_cross = pltpu.make_async_remote_copy(
        src_ref=l_out.at[3], dst_ref=lz_in, send_sem=l_send.at[3], recv_sem=l_recv.at[3],
        device_id=opposite, device_id_type=MESH,
    )

    def prefix_part(k, carry):
        @pl.when(k == 0)
        def _():
            spread_all(0).wait_recv()

        @pl.when(k == 1)
        def _():
            spread_all(1).wait_recv()

        @pl.when(k == 2)
        def _():
            spread_all(2).wait_recv()

        tile = gat[:, k].astype(F32)
        keys = tile[:, 0:8, :].reshape(TOKENS, DH).astype(BF16)
        values = tile[:, 8:16, :].reshape(TOKENS, DH).astype(BF16)
        pre_k[k] = keys
        for c in range(GQA // 2):
            cols = slice(c * PAIR, (c + 1) * PAIR)
            score = dot_last(keys, pair_of(qs, k, c))
            own_peak = stat[k, 0:1, cols]
            peak = jnp.maximum(own_peak, jnp.max(score, axis=0, keepdims=True))
            e = jnp.exp2((score - peak) * EXP_SCALE)
            dprob = dot_last(values, pair_of(dos, k, c))
            shrink = jnp.exp2((own_peak - peak) * EXP_SCALE)
            inverse = 1.0 / (jnp.sum(e, axis=0, keepdims=True) + shrink * stat[k, 1:2, cols])
            delta = (jnp.sum(e * dprob, axis=0, keepdims=True) + shrink * stat[k, 2:3, cols]) * inverse
            scaled = inverse * weight
            prob = e * scaled
            pt[:, cols] = prob.astype(BF16)
            dst[k, 0:TOKENS, cols] = (prob * (dprob - delta)).astype(BF16)
            stat[k, 3:4, cols] = shrink * scaled
            stat[k, 4:5, cols] = delta
        grad_k = dot(dst[k, 0:TOKENS, :], all_of(qs, k)) * FACTOR
        grad_v = dot(pt[...], all_of(dos, k))
        both = jnp.concatenate([grad_k.reshape(PLANE, 8, DH), grad_v.reshape(PLANE, 8, DH)], axis=1)
        part[k] = both[0]
        rs_out[k] = both.astype(BF16)
        for d in range(1, PLANE):
            send(rs_out.at[k, d], rs_in.at[k, d], rs_sems, k, behind[d])

        @pl.when(k >= 2)
        def _():
            plane_sum(k - 2)

        @pl.when(k == 1)
        def _():
            landed(lp_in.at[pl.ds(1, PLANE - 1)], l_sems, 2).wait_recv()
            l_out[3] = l_out[2] + jnp.sum(lp_in[1:PLANE], axis=0)
            length_cross.start()

        return carry

    lax.fori_loop(0, KVH, prefix_part, 0)

    def own_grads(k):
        for c in range(GQA // 2):
            cols = slice(c * PAIR, (c + 1) * PAIR)
            prob = e_own[k, :, cols] * stat[k, 3:4, cols]
            pt[:, cols] = prob.astype(BF16)
            dst[k, TOKENS:PAIR, cols] = (prob * (dp_own[k, :, cols] - stat[k, 4:5, cols])).astype(BF16)
        ogr[k, 0] = dot(dst[k, TOKENS:PAIR, :], all_of(qs, k)) * FACTOR
        ogr[k, 1] = dot(pt[...], all_of(dos, k))

    def own_grads_step(k, carry):
        own_grads(k)
        return carry

    own_grads(0)
    plane_sum(3)
    own_grads(1)
    plane_sum(4)
    lax.fori_loop(2, KVH, own_grads_step, 0)
    length_cross.wait_recv()
    scale = slots / (l_out[3] + lz_in[...])
    scale_out[...] = scale[0:1, 0:1]
    one = scale[0:1, :]
    one_k = one * FACTOR

    def query_grads(k, carry):
        head = pl.ds(pl.multiple_of(k * DH, DH), DH)
        own_t[0, :, head] = (ogr[k, 0] * one).astype(BF16)
        own_t[1, :, head] = (ogr[k, 1] * one).astype(BF16)
        keys = jnp.concatenate([pre_k[k].astype(F32).T, own_k[k].astype(F32).T], axis=1).astype(BF16)
        for c in range(GQA // 2):
            turned = dot(keys, dst[k, :, c * PAIR : (c + 1) * PAIR])
            for g in range(2):
                at = pl.ds(pl.multiple_of(k * WIDTH + (2 * c + g) * DH, DH), DH)
                qg[:, at] = (turned[:, g * DH : (g + 1) * DH].T * one_k).astype(BF16)
        return carry

    lax.fori_loop(0, KVH, query_grads, 0)
    own_out[:, 0, :] = own_t[0]
    own_out[:, 1, :] = own_t[1]

    for k in range(KVH):
        cols = slice(k * DH, (k + 1) * DH)
        cross(k).wait_recv()
        total = (part[k] + zs_in[k].astype(F32)) * one
        pre_out[:, 0, cols] = jnp.where(half == 0, total[0:4], total[4:8])
        pre_out[:, 1, cols] = jnp.where(half == 0, total[8:12], total[12:16])

    for k in range(KVH):
        scatter_all(k).wait_send()
        cross(k).wait_send()
    for at in range(3):
        spread_all(at).wait_send()
    for at in range(2):
        z_copy(at).wait_send()
        landed(la_in.at[pl.ds(1, 3)], l_sems, at).wait_send()
    landed(lp_in.at[pl.ds(1, PLANE - 1)], l_sems, 2).wait_send()
    length_cross.wait_send()


def write_out(qg, own, pre, qg_out, own_out, pre_out, sems):
    copies = [pltpu.make_async_copy(pre, pre_out, sems.at[0])]
    for at in range(8):
        rows = pl.ds(16 * at, 16)
        copies.append(pltpu.make_async_copy(qg.at[rows], qg_out.at[rows], sems.at[1 + at]))
    for at in range(2):
        rows = pl.ds(64 * at, 64)
        copies.append(pltpu.make_async_copy(own.at[rows], own_out.at[rows], sems.at[9 + at]))
    for copy in copies:
        copy.start()
    for copy in copies:
        copy.wait()


def on_device(queries, own_kv, prefix_kv, out_grad, lengths, advantages):
    slots = float(
        queries.shape[2] * lax.axis_size("group") * lax.axis_size("resp") * lax.axis_size("vocab")
    )
    width = KVH * WIDTH
    vmem = pltpu.VMEM
    dma = pltpu.SemaphoreType.DMA
    in_hbm = pl.BlockSpec(memory_space=pltpu.HBM)
    in_smem = pl.BlockSpec(memory_space=pltpu.SMEM)
    in_vmem = pl.BlockSpec(memory_space=pltpu.VMEM)

    def body(*refs):
        kernel(slots, *refs)

    def held(x):
        return pltpu.with_memory_space_constraint(x, pltpu.HBM)

    query_shape, own_shape, prefix_shape = (TOKENS, width), (TOKENS, 2, KVH * DH), (4, 2, KVH * DH)
    query_grad, own_grad, prefix_grad, token_scale = pl.pallas_call(
        body,
        out_shape=(
            vmem(query_shape, BF16),
            vmem(own_shape, BF16),
            vmem(prefix_shape, F32),
            jax.ShapeDtypeStruct((1, 1), F32),
        ),
        in_specs=[in_smem, in_smem, in_hbm, in_hbm, in_hbm, in_hbm],
        out_specs=(in_vmem, in_vmem, in_vmem, in_vmem),
        scratch_shapes=[
            vmem((KVH, TOKENS, WIDTH), BF16),
            vmem((KVH, TOKENS, WIDTH), BF16),
            vmem((TOKENS, 2, KVH * DH), BF16),
            vmem((4, 2, KVH * DH), BF16),
            vmem((KVH, TOKENS, DH), BF16),
            vmem((KVH, TOKENS, DH), BF16),
            vmem((KVH, TOKENS, DH), BF16),
            vmem((KVH, TOKENS, WIDTH), F32),
            vmem((KVH, TOKENS, WIDTH), F32),
            vmem((KVH, 8, WIDTH), F32),
            vmem((TOKENS, WIDTH), BF16),
            vmem((KVH, PAIR, WIDTH), BF16),
            vmem((KVH, 2, TOKENS, DH), F32),
            vmem((2, TOKENS, KVH * DH), BF16),
            vmem((3, 16, DH), BF16),
            vmem((3, 16, DH), BF16),
            vmem((PLANE, KVH, 16, DH), BF16),
            vmem((KVH, PLANE, 16, DH), BF16),
            vmem((KVH, PLANE, 16, DH), BF16),
            vmem((KVH, 16, DH), F32),
            vmem((KVH, 16, DH), BF16),
            vmem((KVH, 16, DH), BF16),
            vmem((4, 8, DH), F32),
            vmem((4, 8, DH), F32),
            vmem((4, 8, DH), F32),
            vmem((PLANE, 8, DH), F32),
            vmem((8, DH), F32),
            dma((2, KVH)),
            dma((2,)),
            dma((2,)),
            dma((2,)),
            dma((3,)),
            dma((3,)),
            dma((KVH,)),
            dma((KVH,)),
            dma((KVH,)),
            dma((KVH,)),
            dma((4,)),
            dma((4,)),
        ],
        compiler_params=pltpu.CompilerParams(
            collective_id=0, has_side_effects=True, vmem_limit_bytes=48 * 1024 * 1024
        ),
        cost_estimate=pl.CostEstimate(
            flops=5 * KVH * 2 * WIDTH * PAIR * DH,
            bytes_accessed=5 * 1024 * 1024,
            transcendentals=KVH * WIDTH * PAIR,
        ),
    )(lengths, advantages, held(queries[0, 0]), held(own_kv[0, 0]), held(prefix_kv[0]), held(out_grad[0, 0]))
    query_grad, own_grad, prefix_grad = pl.pallas_call(
        write_out,
        out_shape=(
            jax.ShapeDtypeStruct(query_shape, BF16),
            jax.ShapeDtypeStruct(own_shape, BF16),
            jax.ShapeDtypeStruct(prefix_shape, F32),
        ),
        in_specs=[in_vmem] * 3,
        out_specs=(in_hbm,) * 3,
        scratch_shapes=[dma((11,))],
        compiler_params=pltpu.CompilerParams(vmem_limit_bytes=8 * 1024 * 1024),
    )(query_grad, own_grad, prefix_grad)
    return query_grad[None, None], own_grad[None, None], prefix_grad[None], token_scale[0, 0]


def solution(mesh):
    in_specs = (
        P("group", ("resp", "vocab"), None, None),
        P("group", ("resp", "vocab"), None, None, None),
        P("group", ("resp", "vocab"), None, None),
        P("group", ("resp", "vocab"), None, None),
        P("group", ("resp", "vocab")),
        P("group", ("resp", "vocab")),
    )
    out_specs = (
        P("group", ("resp", "vocab"), None, None),
        P("group", ("resp", "vocab"), None, None, None),
        P("group", ("resp", "vocab"), None, None),
        P(),
    )
    return jax.shard_map(
        on_device, mesh=mesh, in_specs=in_specs, out_specs=out_specs, check_vma=False
    )
```

time: 60 us -> 53.3 us (0.89)
  local copies, waits for them, and re-layouts: 7.02 us -> 0 us
    unnamed x11 -> x0, local copies, waits for them, and re-layouts: 7.02 us -> none
    pallas_call x1 -> x2, Pallas kernels: 48.4 us -> 48.6 us  [the longest x1 47.3 us: on_device(): pl.pallas_call(body, out_shape=(vmem(query_shape, BF16), vmem(own_shape,...]
where the time goes in v2:
time: 53.3 us; the launch traced here: 52.3 us
  Pallas kernels  48.6 us (91%)
  between operations  3.7 us (7%)
    pallas_call x1, Pallas kernels, on_device(): pl.pallas_call(body, out_shape=(vmem(query_shape, BF16), vmem(own_shape,...  47.3 us
    pallas_call x1, Pallas kernels, on_device(): pl.pallas_call(write_out, out_shape=(jax.ShapeDtypeStruct(query_shape, BF...  1.26 us

profile of v2, /device:TPU:6, one launch (start us, length us, event | category | flops | bytes accessed | tf_op | source)
XLA Modules:
  0.0 52.3 jit_solution(13498718905653981646)
XLA Ops:
  1.9 47.3 %shard_map.93 = (bf16[128,5120]{1,0:T(8,128)(2,1)S(1)}, bf16[128,2,640]{2,1,0:T(2,128)(2,1)S(1)}, f32[4,2,640]{2,1,0:T(2,128)S(1)}, f32[1,1]{1,0:T(1,128)}) custom-call(s32[1,1]{1,0:T(1,128)S(6)} %copy.11.refs_0_, f32[1,1]{1,0:T(1,128)S(6)} %copy.12.refs_1_, bf16[128,5120]{1,0:T(8,128)(2,1)} %bitcast.8, bf16[128,2,640]{2,1,0:T(2,128)(2,1)} %bitcast.11, ...), custom_call_target="tpu_custom_call" | custom-call | flops 1677721600 | bytes 5242880 | tf_op jit(solution)/shard_map/pallas_call | solution.py:373
  49.3 1.3 %shard_map.94 = (bf16[128,5120]{1,0:T(8,128)(2,1)}, bf16[128,2,640]{2,1,0:T(2,128)(2,1)}, f32[4,2,640]{2,1,0:T(2,128)}) custom-call(bf16[128,5120]{1,0:T(8,128)(2,1)S(1)} %get-tuple-element.11.qg, bf16[128,2,640]{2,1,0:T(2,128)(2,1)S(1)} %get-tuple-element.12.own, f32[4,2,640]{2,1,0:T(2,128)S(1)} %get-tuple-element.13.pre), custom_call_target="tpu_custom_call" | custom-call | tf_op jit(solution)/shard_map/pallas_call | solution.py:433

commit v3 on v2

--- a/solution.py
+++ b/solution.py
@@ -13,6 +13,8 @@
 TOKENS = 128
 WIDTH = GQA * DH
 PAIR = 2 * TOKENS
+HALF = 64
+SEEN = TOKENS + HALF
 SIDE = 4
 PLANE = SIDE * SIDE
 FACTOR = 1.0 / math.sqrt(DH)
@@ -37,8 +39,8 @@
     len_ref, adv_ref, q_hbm, own_hbm, pre_hbm, do_hbm,
     qg, own_out, pre_out, scale_out,
     qs, dos, own, pre, own_k, own_v, pre_k, e_own, dp_own, stat, pt, dst, ogr, own_t,
-    z_out, z_in, gat, rs_out, rs_in, part, zs_out, zs_in, l_out, la_in, lb_in, lp_in, lz_in,
-    in_sem, small_sem, z_send, z_recv, g_send, g_recv, rs_send, rs_recv, zs_send, zs_recv, l_send, l_recv,
+    gat_own, gat_far, rs_out, rs_in, part, zs_out, zs_in, l_out, la_in, lb_in, lp_in, lz_in,
+    in_sem, small_sem, z_send, z_recv, go_send, go_recv, gf_send, gf_recv, rs_send, rs_recv, zs_send, zs_recv, l_send, l_recv,
 ):
     group = lax.axis_index("group")
     resp = lax.axis_index("resp")
@@ -88,12 +90,11 @@
     for t in range(3):
         low = mine[2 * t]
         high = mine[2 * t + 1] if 2 * t + 1 < KVH else blank
-        z_out[t] = jnp.concatenate([low, high], axis=0).astype(BF16)
-
-    def z_copy(at):
-        tiles = pl.ds(0, 1) if at == 0 else pl.ds(1, 2)
+        gat_own[t, 0] = jnp.concatenate([low, high], axis=0).astype(BF16)
+
+    def z_copy(t):
         return pltpu.make_async_remote_copy(
-            src_ref=z_out.at[tiles], dst_ref=z_in.at[tiles], send_sem=z_send.at[at], recv_sem=z_recv.at[at],
+            src_ref=gat_own.at[t, 0], dst_ref=gat_far.at[t, 0], send_sem=z_send.at[t], recv_sem=z_recv.at[t],
             device_id=opposite, device_id_type=MESH,
         )
 
@@ -109,11 +110,14 @@
             device_id=opposite, device_id_type=MESH,
         )
 
-    g_sems, l_sems, rs_sems = (g_send, g_recv), (l_send, l_recv), (rs_send, rs_recv)
+    go_sems, gf_sems = (go_send, go_recv), (gf_send, gf_recv)
+    l_sems, rs_sems = (l_send, l_recv), (rs_send, rs_recv)
 
     pl.semaphore_wait(barrier, len(partners))
-    z_copy(0).start()
-    z_copy(1).start()
+    for t in range(3):
+        z_copy(t).start()
+    for d in range(1, PLANE):
+        send(gat_own.at[:, 0], gat_own.at[:, d], go_sems, 0, ahead[d])
     for o in range(1, 4):
         send(l_out.at[0], la_in.at[o], l_sems, 0, near[o])
 
@@ -127,9 +131,9 @@
 
     lane = lax.broadcasted_iota(jnp.int32, (1, PAIR), 1) % TOKENS
     weight = jnp.where(lane < length, adv_ref[0, 0], 0.0)
-    key_at = lax.broadcasted_iota(jnp.int32, (TOKENS, PAIR), 0)
-    query_at = lax.broadcasted_iota(jnp.int32, (TOKENS, PAIR), 1) % TOKENS
-    causal = key_at <= query_at
+    key_at = lax.broadcasted_iota(jnp.int32, (SEEN, PAIR), 0)
+    query_at = lax.broadcasted_iota(jnp.int32, (SEEN, PAIR), 1) % TOKENS
+    causal = (key_at <= query_at) | (key_at >= TOKENS)
 
     def pair_of(ref, k, c):
         return jnp.concatenate(
@@ -139,11 +143,20 @@
     def all_of(ref, k):
         return jnp.concatenate([ref[k, :, g * DH : (g + 1) * DH] for g in range(GQA)], axis=0)
 
+    def rows_of(ref, k):
+        tile = ref[k // 2].astype(F32)
+        tile = jnp.where(k % 2 == 0, tile[:, 0:8, :], tile[:, 8:16, :])
+        keys = [tile[s, 0:4] for s in range(PLANE)]
+        values = [tile[s, 4:8] for s in range(PLANE)]
+        return jnp.concatenate(keys, axis=0).astype(BF16), jnp.concatenate(values, axis=0).astype(BF16)
+
     def own_part(k):
         for copy in in_copies(k):
             copy.wait()
-        keys = own_k[k]
-        values = own_v[k]
+        plane_keys, plane_values = rows_of(gat_own, k)
+        pre_k[k, 0:HALF] = plane_keys
+        keys = jnp.concatenate([own_k[k], plane_keys], axis=0)
+        values = jnp.concatenate([own_v[k], plane_values], axis=0)
         for c in range(GQA // 2):
             cols = slice(c * PAIR, (c + 1) * PAIR)
             score = jnp.where(causal, dot_last(keys, pair_of(qs, k, c)), LOW)
@@ -163,45 +176,31 @@
 
         lax.fori_loop(start, stop, step, 0)
 
-    def unit(k):
-        at, rows = k // 2, slice(8 * (k % 2), 8 * (k % 2) + 8)
-        here = z_out[at].astype(F32)[rows]
-        there = z_in[at].astype(F32)[rows]
-        first = jnp.where(half == 0, here, there)
-        second = jnp.where(half == 0, there, here)
-        gat[0, k] = jnp.concatenate([first[0:4], second[0:4], first[4:8], second[4:8]], axis=0).astype(BF16)
-
-    parts = ((0, 1), (1, 1), (2, 3))
-
-    def spread(at):
-        start, count = parts[at]
+    def spread_own_all():
+        return landed(gat_own.at[:, pl.ds(1, PLANE - 1)], go_sems, 0)
+
+    def spread(t):
+        z_copy(t).wait_recv()
         for d in range(1, PLANE):
-            send(gat.at[0, pl.ds(start, count)], gat.at[d, pl.ds(start, count)], g_sems, at, ahead[d])
-
-    def spread_all(at):
-        start, count = parts[at]
-        return landed(gat.at[pl.ds(1, PLANE - 1), pl.ds(start, count)], g_sems, at)
-
-    own_part(0)
+            send(gat_far.at[t, 0], gat_far.at[t, d], gf_sems, t, ahead[d])
+
+    def spread_all(t):
+        return landed(gat_far.at[t, pl.ds(1, PLANE - 1)], gf_sems, t)
+
     landed(la_in.at[pl.ds(1, 3)], l_sems, 0).wait_recv()
     l_out[1] = l_out[0] + la_in[1] + la_in[2] + la_in[3]
     for o in range(1, 4):
         send(l_out.at[1], lb_in.at[o], l_sems, 1, far[o])
-    own_parts(1, 3)
-    z_copy(0).wait_recv()
-    unit(0)
-    spread(0)
-    unit(1)
-    spread(1)
-    z_copy(1).wait_recv()
-    for k in range(2, KVH):
-        unit(k)
-    spread(2)
+    spread_own_all().wait_recv()
+    own_part(0)
+    for t in range(3):
+        spread(t)
+    own_parts(1, 2)
     landed(lb_in.at[pl.ds(1, 3)], l_sems, 1).wait_recv()
     l_out[2] = l_out[1] + lb_in[1] + lb_in[2] + lb_in[3]
     for d in range(1, PLANE):
         send(l_out.at[2], lp_in.at[d], l_sems, 2, ahead[d])
-    own_parts(3, KVH)
+    own_parts(2, KVH)
 
     def scatter_all(k):
         return landed(rs_out.at[k, pl.ds(1, PLANE - 1)], rs_sems, k)
@@ -229,18 +228,16 @@
         def _():
             spread_all(0).wait_recv()
 
-        @pl.when(k == 1)
+        @pl.when(k == 2)
         def _():
             spread_all(1).wait_recv()
 
-        @pl.when(k == 2)
+        @pl.when(k == 4)
         def _():
             spread_all(2).wait_recv()
 
-        tile = gat[:, k].astype(F32)
-        keys = tile[:, 0:8, :].reshape(TOKENS, DH).astype(BF16)
-        values = tile[:, 8:16, :].reshape(TOKENS, DH).astype(BF16)
-        pre_k[k] = keys
+        keys, values = rows_of(gat_far, k)
+        pre_k[k, HALF:TOKENS] = keys
         for c in range(GQA // 2):
             cols = slice(c * PAIR, (c + 1) * PAIR)
             score = dot_last(keys, pair_of(qs, k, c))
@@ -252,16 +249,26 @@
             inverse = 1.0 / (jnp.sum(e, axis=0, keepdims=True) + shrink * stat[k, 1:2, cols])
             delta = (jnp.sum(e * dprob, axis=0, keepdims=True) + shrink * stat[k, 2:3, cols]) * inverse
             scaled = inverse * weight
-            prob = e * scaled
-            pt[:, cols] = prob.astype(BF16)
-            dst[k, 0:TOKENS, cols] = (prob * (dprob - delta)).astype(BF16)
-            stat[k, 3:4, cols] = shrink * scaled
+            own_scaled = shrink * scaled
+            near_prob = e_own[k, TOKENS:SEEN, cols] * own_scaled
+            far_prob = e * scaled
+            pt[0:HALF, cols] = near_prob.astype(BF16)
+            pt[HALF:TOKENS, cols] = far_prob.astype(BF16)
+            dst[k, 0:HALF, cols] = (near_prob * (dp_own[k, TOKENS:SEEN, cols] - delta)).astype(BF16)
+            dst[k, HALF:TOKENS, cols] = (far_prob * (dprob - delta)).astype(BF16)
+            stat[k, 3:4, cols] = own_scaled
             stat[k, 4:5, cols] = delta
         grad_k = dot(dst[k, 0:TOKENS, :], all_of(qs, k)) * FACTOR
         grad_v = dot(pt[...], all_of(dos, k))
-        both = jnp.concatenate([grad_k.reshape(PLANE, 8, DH), grad_v.reshape(PLANE, 8, DH)], axis=1)
-        part[k] = both[0]
-        rs_out[k] = both.astype(BF16)
+        for d in range(PLANE):
+            near_rows, far_rows = slice(4 * d, 4 * d + 4), slice(HALF + 4 * d, HALF + 4 * d + 4)
+            tile = jnp.concatenate(
+                [grad_k[near_rows], grad_k[far_rows], grad_v[near_rows], grad_v[far_rows]], axis=0
+            )
+            if d == 0:
+                part[k] = tile
+            else:
+                rs_out[k, d] = tile.astype(BF16)
         for d in range(1, PLANE):
             send(rs_out.at[k, d], rs_in.at[k, d], rs_sems, k, behind[d])
 
@@ -282,9 +289,9 @@
     def own_grads(k):
         for c in range(GQA // 2):
             cols = slice(c * PAIR, (c + 1) * PAIR)
-            prob = e_own[k, :, cols] * stat[k, 3:4, cols]
+            prob = e_own[k, 0:TOKENS, cols] * stat[k, 3:4, cols]
             pt[:, cols] = prob.astype(BF16)
-            dst[k, TOKENS:PAIR, cols] = (prob * (dp_own[k, :, cols] - stat[k, 4:5, cols])).astype(BF16)
+            dst[k, TOKENS:PAIR, cols] = (prob * (dp_own[k, 0:TOKENS, cols] - stat[k, 4:5, cols])).astype(BF16)
         ogr[k, 0] = dot(dst[k, TOKENS:PAIR, :], all_of(qs, k)) * FACTOR
         ogr[k, 1] = dot(pt[...], all_of(dos, k))
 
@@ -322,17 +329,18 @@
     for k in range(KVH):
         cols = slice(k * DH, (k + 1) * DH)
         cross(k).wait_recv()
-        total = (part[k] + zs_in[k].astype(F32)) * one
-        pre_out[:, 0, cols] = jnp.where(half == 0, total[0:4], total[4:8])
-        pre_out[:, 1, cols] = jnp.where(half == 0, total[8:12], total[12:16])
+        there = zs_in[k].astype(F32)
+        pre_out[:, 0, cols] = (part[k, 0:4] + there[4:8]) * one
+        pre_out[:, 1, cols] = (part[k, 8:12] + there[12:16]) * one
 
     for k in range(KVH):
         scatter_all(k).wait_send()
         cross(k).wait_send()
-    for at in range(3):
-        spread_all(at).wait_send()
+    spread_own_all().wait_send()
+    for t in range(3):
+        spread_all(t).wait_send()
+        z_copy(t).wait_send()
     for at in range(2):
-        z_copy(at).wait_send()
         landed(la_in.at[pl.ds(1, 3)], l_sems, at).wait_send()
     landed(lp_in.at[pl.ds(1, PLANE - 1)], l_sems, 2).wait_send()
     length_cross.wait_send()
@@ -388,16 +396,15 @@
             vmem((KVH, TOKENS, DH), BF16),
             vmem((KVH, TOKENS, DH), BF16),
             vmem((KVH, TOKENS, DH), BF16),
-            vmem((KVH, TOKENS, WIDTH), F32),
-            vmem((KVH, TOKENS, WIDTH), F32),
+            vmem((KVH, SEEN, WIDTH), F32),
+            vmem((KVH, SEEN, WIDTH), F32),
             vmem((KVH, 8, WIDTH), F32),
             vmem((TOKENS, WIDTH), BF16),
             vmem((KVH, PAIR, WIDTH), BF16),
             vmem((KVH, 2, TOKENS, DH), F32),
             vmem((2, TOKENS, KVH * DH), BF16),
-            vmem((3, 16, DH), BF16),
-            vmem((3, 16, DH), BF16),
-            vmem((PLANE, KVH, 16, DH), BF16),
+            vmem((3, PLANE, 16, DH), BF16),
+            vmem((3, PLANE, 16, DH), BF16),
             vmem((KVH, PLANE, 16, DH), BF16),
             vmem((KVH, PLANE, 16, DH), BF16),
             vmem((KVH, 16, DH), F32),
@@ -410,8 +417,10 @@
             vmem((8, DH), F32),
             dma((2, KVH)),
             dma((2,)),
-            dma((2,)),
-            dma((2,)),
+            dma((3,)),
+            dma((3,)),
+            dma((1,)),
+            dma((1,)),
             dma((3,)),
             dma((3,)),
             dma((KVH,)),

time: 53.3 us -> 53.1 us (level)
  no operation moved by 1% of the time
where the time goes in v3:
time: 53.1 us; the launch traced here: 52.2 us
  Pallas kernels  48.5 us (91%)
  between operations  3.7 us (7%)
    pallas_call x1, Pallas kernels, on_device(): pl.pallas_call(body, out_shape=(vmem(query_shape, BF16), vmem(own_shape,...  47.3 us
    pallas_call x1, Pallas kernels, on_device(): pl.pallas_call(write_out, out_shape=(jax.ShapeDtypeStruct(query_shape, BF...  1.26 us

profile of v3, /device:TPU:6, one launch (start us, length us, event | category | flops | bytes accessed | tf_op | source)
XLA Modules:
  0.0 52.2 jit_solution(17429998435705639780)
XLA Ops:
  1.9 47.3 %shard_map.93 = (bf16[128,5120]{1,0:T(8,128)(2,1)S(1)}, bf16[128,2,640]{2,1,0:T(2,128)(2,1)S(1)}, f32[4,2,640]{2,1,0:T(2,128)S(1)}, f32[1,1]{1,0:T(1,128)}) custom-call(s32[1,1]{1,0:T(1,128)S(6)} %copy.11.refs_0_, f32[1,1]{1,0:T(1,128)S(6)} %copy.12.refs_1_, bf16[128,5120]{1,0:T(8,128)(2,1)} %bitcast.8, bf16[128,2,640]{2,1,0:T(2,128)(2,1)} %bitcast.11, ...), custom_call_target="tpu_custom_call" | custom-call | flops 1677721600 | bytes 5242880 | tf_op jit(solution)/shard_map/pallas_call | solution.py:381
  49.2 1.3 %shard_map.94 = (bf16[128,5120]{1,0:T(8,128)(2,1)}, bf16[128,2,640]{2,1,0:T(2,128)(2,1)}, f32[4,2,640]{2,1,0:T(2,128)}) custom-call(bf16[128,5120]{1,0:T(8,128)(2,1)S(1)} %get-tuple-element.11.qg, bf16[128,2,640]{2,1,0:T(2,128)(2,1)S(1)} %get-tuple-element.12.own, f32[4,2,640]{2,1,0:T(2,128)S(1)} %get-tuple-element.13.pre), custom_call_target="tpu_custom_call" | custom-call | tf_op jit(solution)/shard_map/pallas_call | solution.py:442

commit v4 on v3

--- a/solution.py
+++ b/solution.py
@@ -39,7 +39,7 @@
     len_ref, adv_ref, q_hbm, own_hbm, pre_hbm, do_hbm,
     qg, own_out, pre_out, scale_out,
     qs, dos, own, pre, own_k, own_v, pre_k, e_own, dp_own, stat, pt, dst, ogr, own_t,
-    gat_own, gat_far, rs_out, rs_in, part, zs_out, zs_in, l_out, la_in, lb_in, lp_in, lz_in,
+    gat_own, gat_far, rs_out, rs_in, part, zs_out, zs_in, l_out, la_in, lb_in, lp_in,
     in_sem, small_sem, z_send, z_recv, go_send, go_recv, gf_send, gf_recv, rs_send, rs_recv, zs_send, zs_recv, l_send, l_recv,
 ):
     group = lax.axis_index("group")
@@ -56,9 +56,10 @@
     opposite = (group, row * 2 + 1 - half, vocab)
     near = [None] + [((group // 4) * 4 + (group + o) % 4, resp, vocab) for o in range(1, 4)]
     far = [None] + [((group + 4 * o) % 16, resp, vocab) for o in range(1, 4)]
+    far += [((group + 4 * o) % 16, row * 2 + 1 - half, vocab) for o in range(4)]
 
     barrier = pltpu.get_barrier_semaphore()
-    partners = [opposite] + ahead[1:] + near[1:] + far[1:]
+    partners = [opposite] + ahead[1:] + near[1:] + far[1:4] + far[5:]
     for partner in partners:
         pl.semaphore_signal(barrier, inc=1, device_id=partner, device_id_type=MESH)
 
@@ -189,18 +190,18 @@
 
     landed(la_in.at[pl.ds(1, 3)], l_sems, 0).wait_recv()
     l_out[1] = l_out[0] + la_in[1] + la_in[2] + la_in[3]
-    for o in range(1, 4):
+    for o in range(1, 8):
         send(l_out.at[1], lb_in.at[o], l_sems, 1, far[o])
     spread_own_all().wait_recv()
     own_part(0)
     for t in range(3):
         spread(t)
-    own_parts(1, 2)
-    landed(lb_in.at[pl.ds(1, 3)], l_sems, 1).wait_recv()
-    l_out[2] = l_out[1] + lb_in[1] + lb_in[2] + lb_in[3]
+    own_parts(1, 3)
+    landed(lb_in.at[pl.ds(1, 7)], l_sems, 1).wait_recv()
+    l_out[2] = l_out[1] + jnp.sum(lb_in[1:8], axis=0)
     for d in range(1, PLANE):
         send(l_out.at[2], lp_in.at[d], l_sems, 2, ahead[d])
-    own_parts(2, KVH)
+    own_parts(3, KVH)
 
     def scatter_all(k):
         return landed(rs_out.at[k, pl.ds(1, PLANE - 1)], rs_sems, k)
@@ -217,11 +218,6 @@
         part[k] = total
         zs_out[k] = total.astype(BF16)
         cross(k).start()
-
-    length_cross = pltpu.make_async_remote_copy(
-        src_ref=l_out.at[3], dst_ref=lz_in, send_sem=l_send.at[3], recv_sem=l_recv.at[3],
-        device_id=opposite, device_id_type=MESH,
-    )
 
     def prefix_part(k, carry):
         @pl.when(k == 0)
@@ -272,16 +268,6 @@
         for d in range(1, PLANE):
             send(rs_out.at[k, d], rs_in.at[k, d], rs_sems, k, behind[d])
 
-        @pl.when(k >= 2)
-        def _():
-            plane_sum(k - 2)
-
-        @pl.when(k == 1)
-        def _():
-            landed(lp_in.at[pl.ds(1, PLANE - 1)], l_sems, 2).wait_recv()
-            l_out[3] = l_out[2] + jnp.sum(lp_in[1:PLANE], axis=0)
-            length_cross.start()
-
         return carry
 
     lax.fori_loop(0, KVH, prefix_part, 0)
@@ -299,14 +285,18 @@
         own_grads(k)
         return carry
 
-    own_grads(0)
-    plane_sum(3)
-    own_grads(1)
-    plane_sum(4)
-    lax.fori_loop(2, KVH, own_grads_step, 0)
-    length_cross.wait_recv()
-    scale = slots / (l_out[3] + lz_in[...])
-    scale_out[...] = scale[0:1, 0:1]
+    def plane_sum_step(k, carry):
+        plane_sum(k)
+        return carry
+
+    lax.fori_loop(0, 3, own_grads_step, 0)
+    lax.fori_loop(0, 3, plane_sum_step, 0)
+    lax.fori_loop(3, 4, own_grads_step, 0)
+    lax.fori_loop(3, KVH, plane_sum_step, 0)
+    lax.fori_loop(4, KVH, own_grads_step, 0)
+    landed(lp_in.at[pl.ds(1, PLANE - 1)], l_sems, 2).wait_recv()
+    scale = slots / (l_out[2] + jnp.sum(lp_in[1:PLANE], axis=0))
+    scale_out[...] = scale
     one = scale[0:1, :]
     one_k = one * FACTOR
 
@@ -340,14 +330,17 @@
     for t in range(3):
         spread_all(t).wait_send()
         z_copy(t).wait_send()
-    for at in range(2):
-        landed(la_in.at[pl.ds(1, 3)], l_sems, at).wait_send()
+    landed(la_in.at[pl.ds(1, 3)], l_sems, 0).wait_send()
+    landed(lb_in.at[pl.ds(1, 7)], l_sems, 1).wait_send()
     landed(lp_in.at[pl.ds(1, PLANE - 1)], l_sems, 2).wait_send()
-    length_cross.wait_send()
-
-
-def write_out(qg, own, pre, qg_out, own_out, pre_out, sems):
-    copies = [pltpu.make_async_copy(pre, pre_out, sems.at[0])]
+
+
+def write_out(qg, own, pre, scale, qg_out, own_out, pre_out, scale_out, one, sems):
+    one[...] = scale[0:1, 0:1]
+    copies = [
+        pltpu.make_async_copy(pre, pre_out, sems.at[0]),
+        pltpu.make_async_copy(one, scale_out, sems.at[11]),
+    ]
     for at in range(8):
         rows = pl.ds(16 * at, 16)
         copies.append(pltpu.make_async_copy(qg.at[rows], qg_out.at[rows], sems.at[1 + at]))
@@ -384,7 +377,7 @@
             vmem(query_shape, BF16),
             vmem(own_shape, BF16),
             vmem(prefix_shape, F32),
-            jax.ShapeDtypeStruct((1, 1), F32),
+            vmem((8, DH), F32),
         ),
         in_specs=[in_smem, in_smem, in_hbm, in_hbm, in_hbm, in_hbm],
         out_specs=(in_vmem, in_vmem, in_vmem, in_vmem),
@@ -410,11 +403,10 @@
             vmem((KVH, 16, DH), F32),
             vmem((KVH, 16, DH), BF16),
             vmem((KVH, 16, DH), BF16),
+            vmem((3, 8, DH), F32),
             vmem((4, 8, DH), F32),
-            vmem((4, 8, DH), F32),
-            vmem((4, 8, DH), F32),
+            vmem((8, 8, DH), F32),
             vmem((PLANE, 8, DH), F32),
-            vmem((8, DH), F32),
             dma((2, KVH)),
             dma((2,)),
             dma((3,)),
@@ -427,8 +419,8 @@
             dma((KVH,)),
             dma((KVH,)),
             dma((KVH,)),
-            dma((4,)),
-            dma((4,)),
+            dma((3,)),
+            dma((3,)),
         ],
         compiler_params=pltpu.CompilerParams(
             collective_id=0, has_side_effects=True, vmem_limit_bytes=48 * 1024 * 1024
@@ -439,18 +431,19 @@
             transcendentals=KVH * WIDTH * PAIR,
         ),
     )(lengths, advantages, held(queries[0, 0]), held(own_kv[0, 0]), held(prefix_kv[0]), held(out_grad[0, 0]))
-    query_grad, own_grad, prefix_grad = pl.pallas_call(
+    query_grad, own_grad, prefix_grad, token_scale = pl.pallas_call(
         write_out,
         out_shape=(
             jax.ShapeDtypeStruct(query_shape, BF16),
             jax.ShapeDtypeStruct(own_shape, BF16),
             jax.ShapeDtypeStruct(prefix_shape, F32),
+            jax.ShapeDtypeStruct((1, 1), F32),
         ),
-        in_specs=[in_vmem] * 3,
-        out_specs=(in_hbm,) * 3,
-        scratch_shapes=[dma((11,))],
+        in_specs=[in_vmem] * 4,
+        out_specs=(in_hbm,) * 4,
+        scratch_shapes=[vmem((1, 1), F32), dma((12,))],
         compiler_params=pltpu.CompilerParams(vmem_limit_bytes=8 * 1024 * 1024),
-    )(query_grad, own_grad, prefix_grad)
+    )(query_grad, own_grad, prefix_grad, token_scale)
     return query_grad[None, None], own_grad[None, None], prefix_grad[None], token_scale[0, 0]
 
 

time: 53.1 us -> 46.8 us (0.88); the launches traced: 52.2 us -> 46.6 us
  Pallas kernels: 48.5 us -> 44.6 us
  between operations: 3.7 us -> 1.93 us
    pallas_call x1, Pallas kernels: 47.3 us -> 43.4 us  [on_device(): pl.pallas_call(body, out_shape=(vmem(query_shape, BF16), vmem(own_shape,...]
where the time goes in v4:
time: 46.8 us; the launch traced here: 46.6 us
  Pallas kernels  44.6 us (95%)
  between operations  1.93 us (4%)
    pallas_call x1, Pallas kernels, on_device(): pl.pallas_call(body, out_shape=(vmem(query_shape, BF16), vmem(own_shape,...  43.4 us
    pallas_call x1, Pallas kernels, on_device(): pl.pallas_call(write_out, out_shape=(jax.ShapeDtypeStruct(query_shape, BF...  1.27 us

profile of v4, /device:TPU:6, one launch (start us, length us, event | category | flops | bytes accessed | tf_op | source)
XLA Modules:
  0.0 46.6 jit_solution(11500202498244185551)
XLA Ops:
  1.9 43.4 %shard_map.93 = (bf16[128,5120]{1,0:T(8,128)(2,1)S(1)}, bf16[128,2,640]{2,1,0:T(2,128)(2,1)S(1)}, f32[4,2,640]{2,1,0:T(2,128)S(1)}, f32[8,128]{1,0:T(8,128)S(1)}) custom-call(s32[1,1]{1,0:T(1,128)S(6)} %copy.10.refs_0_, f32[1,1]{1,0:T(1,128)S(6)} %copy.11.refs_1_, bf16[128,5120]{1,0:T(8,128)(2,1)} %bitcast.8, bf16[128,2,640]{2,1,0:T(2,128)(2,1)} %bitcast.11, ...), custom_call_target="tpu_custom_call" | custom-call | flops 1677721600 | bytes 5242880 | tf_op jit(solution)/shard_map/pallas_call | solution.py:374
  45.3 1.3 %shard_map.94 = (bf16[128,5120]{1,0:T(8,128)(2,1)}, bf16[128,2,640]{2,1,0:T(2,128)(2,1)}, f32[4,2,640]{2,1,0:T(2,128)}, f32[1,1]{1,0:T(1,128)}) custom-call(bf16[128,5120]{1,0:T(8,128)(2,1)S(1)} %get-tuple-element.12.qg, bf16[128,2,640]{2,1,0:T(2,128)(2,1)S(1)} %get-tuple-element.13.own, f32[4,2,640]{2,1,0:T(2,128)S(1)} %get-tuple-element.14.pre, ...), custom_call_target="tpu_custom_call" | custom-call | tf_op jit(solution)/shard_map/pallas_call | solution.py:434

commit v5 on v4

--- a/solution.py
+++ b/solution.py
@@ -132,9 +132,9 @@
 
     lane = lax.broadcasted_iota(jnp.int32, (1, PAIR), 1) % TOKENS
     weight = jnp.where(lane < length, adv_ref[0, 0], 0.0)
-    key_at = lax.broadcasted_iota(jnp.int32, (SEEN, PAIR), 0)
-    query_at = lax.broadcasted_iota(jnp.int32, (SEEN, PAIR), 1) % TOKENS
-    causal = (key_at <= query_at) | (key_at >= TOKENS)
+    key_at = lax.broadcasted_iota(jnp.int32, (TOKENS, PAIR), 0)
+    query_at = lax.broadcasted_iota(jnp.int32, (TOKENS, PAIR), 1) % TOKENS
+    causal = key_at <= query_at
 
     def pair_of(ref, k, c):
         return jnp.concatenate(
@@ -151,24 +151,31 @@
         values = [tile[s, 4:8] for s in range(PLANE)]
         return jnp.concatenate(keys, axis=0).astype(BF16), jnp.concatenate(values, axis=0).astype(BF16)
 
+    def seen_part(k, rows, keys, values, mask, at):
+        for c in range(GQA // 2):
+            cols = slice(c * PAIR, (c + 1) * PAIR)
+            score = dot_last(keys, pair_of(qs, k, c))
+            if mask is not None:
+                score = jnp.where(mask, score, LOW)
+            peak = jnp.max(score, axis=0, keepdims=True)
+            e = jnp.exp2((score - peak) * EXP_SCALE)
+            dprob = dot_last(values, pair_of(dos, k, c))
+            e_own[k, rows, cols] = e
+            dp_own[k, rows, cols] = dprob
+            stat[k, at : at + 1, cols] = peak
+            stat[k, at + 1 : at + 2, cols] = jnp.sum(e, axis=0, keepdims=True)
+            stat[k, at + 2 : at + 3, cols] = jnp.sum(e * dprob, axis=0, keepdims=True)
+
     def own_part(k):
         for copy in in_copies(k):
             copy.wait()
-        plane_keys, plane_values = rows_of(gat_own, k)
-        pre_k[k, 0:HALF] = plane_keys
-        keys = jnp.concatenate([own_k[k], plane_keys], axis=0)
-        values = jnp.concatenate([own_v[k], plane_values], axis=0)
-        for c in range(GQA // 2):
-            cols = slice(c * PAIR, (c + 1) * PAIR)
-            score = jnp.where(causal, dot_last(keys, pair_of(qs, k, c)), LOW)
-            peak = jnp.max(score, axis=0, keepdims=True)
-            e = jnp.exp2((score - peak) * EXP_SCALE)
-            dprob = dot_last(values, pair_of(dos, k, c))
-            e_own[k, :, cols] = e
-            dp_own[k, :, cols] = dprob
-            stat[k, 0:1, cols] = peak
-            stat[k, 1:2, cols] = jnp.sum(e, axis=0, keepdims=True)
-            stat[k, 2:3, cols] = jnp.sum(e * dprob, axis=0, keepdims=True)
+        seen_part(k, slice(0, TOKENS), own_k[k], own_v[k], causal, 0)
+
+    def plane_part(k, carry):
+        keys, values = rows_of(gat_own, k)
+        pre_k[k, 0:HALF] = keys
+        seen_part(k, slice(TOKENS, SEEN), keys, values, None, 5)
+        return carry
 
     def own_parts(start, stop):
         def step(k, carry):
@@ -188,20 +195,16 @@
     def spread_all(t):
         return landed(gat_far.at[t, pl.ds(1, PLANE - 1)], gf_sems, t)
 
+    own_parts(0, 1)
     landed(la_in.at[pl.ds(1, 3)], l_sems, 0).wait_recv()
     l_out[1] = l_out[0] + la_in[1] + la_in[2] + la_in[3]
     for o in range(1, 8):
         send(l_out.at[1], lb_in.at[o], l_sems, 1, far[o])
-    spread_own_all().wait_recv()
-    own_part(0)
+    own_parts(1, KVH)
     for t in range(3):
         spread(t)
-    own_parts(1, 3)
-    landed(lb_in.at[pl.ds(1, 7)], l_sems, 1).wait_recv()
-    l_out[2] = l_out[1] + jnp.sum(lb_in[1:8], axis=0)
-    for d in range(1, PLANE):
-        send(l_out.at[2], lp_in.at[d], l_sems, 2, ahead[d])
-    own_parts(3, KVH)
+    spread_own_all().wait_recv()
+    lax.fori_loop(0, KVH, plane_part, 0)
 
     def scatter_all(k):
         return landed(rs_out.at[k, pl.ds(1, PLANE - 1)], rs_sems, k)
@@ -237,16 +240,19 @@
         for c in range(GQA // 2):
             cols = slice(c * PAIR, (c + 1) * PAIR)
             score = dot_last(keys, pair_of(qs, k, c))
-            own_peak = stat[k, 0:1, cols]
-            peak = jnp.maximum(own_peak, jnp.max(score, axis=0, keepdims=True))
+            own_peak, near_peak = stat[k, 0:1, cols], stat[k, 5:6, cols]
+            peak = jnp.maximum(jnp.maximum(own_peak, near_peak), jnp.max(score, axis=0, keepdims=True))
             e = jnp.exp2((score - peak) * EXP_SCALE)
             dprob = dot_last(values, pair_of(dos, k, c))
             shrink = jnp.exp2((own_peak - peak) * EXP_SCALE)
-            inverse = 1.0 / (jnp.sum(e, axis=0, keepdims=True) + shrink * stat[k, 1:2, cols])
-            delta = (jnp.sum(e * dprob, axis=0, keepdims=True) + shrink * stat[k, 2:3, cols]) * inverse
+            near_shrink = jnp.exp2((near_peak - peak) * EXP_SCALE)
+            total = shrink * stat[k, 1:2, cols] + near_shrink * stat[k, 6:7, cols]
+            inverse = 1.0 / (jnp.sum(e, axis=0, keepdims=True) + total)
+            products = shrink * stat[k, 2:3, cols] + near_shrink * stat[k, 7:8, cols]
+            delta = (jnp.sum(e * dprob, axis=0, keepdims=True) + products) * inverse
             scaled = inverse * weight
             own_scaled = shrink * scaled
-            near_prob = e_own[k, TOKENS:SEEN, cols] * own_scaled
+            near_prob = e_own[k, TOKENS:SEEN, cols] * (near_shrink * scaled)
             far_prob = e * scaled
             pt[0:HALF, cols] = near_prob.astype(BF16)
             pt[HALF:TOKENS, cols] = far_prob.astype(BF16)
@@ -267,6 +273,13 @@
                 rs_out[k, d] = tile.astype(BF16)
         for d in range(1, PLANE):
             send(rs_out.at[k, d], rs_in.at[k, d], rs_sems, k, behind[d])
+
+        @pl.when(k == 1)
+        def _():
+            landed(lb_in.at[pl.ds(1, 7)], l_sems, 1).wait_recv()
+            l_out[2] = l_out[1] + jnp.sum(lb_in[1:8], axis=0)
+            for d in range(1, PLANE):
+                send(l_out.at[2], lp_in.at[d], l_sems, 2, ahead[d])
 
         return carry
 

time: 46.8 us -> 46.9 us (level)
  no operation moved by 1% of the time
where the time goes in v5:
time: 46.9 us; the launch traced here: 46.7 us
  Pallas kernels  44.8 us (96%)
  between operations  1.93 us (4%)
    pallas_call x1, Pallas kernels, on_device(): pl.pallas_call(body, out_shape=(vmem(query_shape, BF16), vmem(own_shape,...  43.5 us
    pallas_call x1, Pallas kernels, on_device(): pl.pallas_call(write_out, out_shape=(jax.ShapeDtypeStruct(query_shape, BF...  1.27 us

profile of v5, /device:TPU:6, one launch (start us, length us, event | category | flops | bytes accessed | tf_op | source)
XLA Modules:
  0.0 46.7 jit_solution(15970201986000601809)
XLA Ops:
  1.9 43.5 %shard_map.93 = (bf16[128,5120]{1,0:T(8,128)(2,1)S(1)}, bf16[128,2,640]{2,1,0:T(2,128)(2,1)S(1)}, f32[4,2,640]{2,1,0:T(2,128)S(1)}, f32[8,128]{1,0:T(8,128)S(1)}) custom-call(s32[1,1]{1,0:T(1,128)S(6)} %copy.10.refs_0_, f32[1,1]{1,0:T(1,128)S(6)} %copy.11.refs_1_, bf16[128,5120]{1,0:T(8,128)(2,1)} %bitcast.8, bf16[128,2,640]{2,1,0:T(2,128)(2,1)} %bitcast.11, ...), custom_call_target="tpu_custom_call" | custom-call | flops 1677721600 | bytes 5242880 | tf_op jit(solution)/shard_map/pallas_call | solution.py:387
  45.5 1.3 %shard_map.94 = (bf16[128,5120]{1,0:T(8,128)(2,1)}, bf16[128,2,640]{2,1,0:T(2,128)(2,1)}, f32[4,2,640]{2,1,0:T(2,128)}, f32[1,1]{1,0:T(1,128)}) custom-call(bf16[128,5120]{1,0:T(8,128)(2,1)S(1)} %get-tuple-element.12.qg, bf16[128,2,640]{2,1,0:T(2,128)(2,1)S(1)} %get-tuple-element.13.own, f32[4,2,640]{2,1,0:T(2,128)S(1)} %get-tuple-element.14.pre, ...), custom_call_target="tpu_custom_call" | custom-call | tf_op jit(solution)/shard_map/pallas_call | solution.py:447

commit v6 on v5

--- a/solution.py
+++ b/solution.py
@@ -200,9 +200,10 @@
     l_out[1] = l_out[0] + la_in[1] + la_in[2] + la_in[3]
     for o in range(1, 8):
         send(l_out.at[1], lb_in.at[o], l_sems, 1, far[o])
-    own_parts(1, KVH)
+    own_parts(1, 3)
     for t in range(3):
         spread(t)
+    own_parts(3, KVH)
     spread_own_all().wait_recv()
     lax.fori_loop(0, KVH, plane_part, 0)
 

time: 46.9 us -> 47 us (level)
  no operation moved by 1% of the time
where the time goes in v6:
time: 47 us; the launch traced here: 46.8 us
  Pallas kernels  44.9 us (96%)
  between operations  1.93 us (4%)
    pallas_call x1, Pallas kernels, on_device(): pl.pallas_call(body, out_shape=(vmem(query_shape, BF16), vmem(own_shape,...  43.6 us
    pallas_call x1, Pallas kernels, on_device(): pl.pallas_call(write_out, out_shape=(jax.ShapeDtypeStruct(query_shape, BF...  1.27 us

profile of v6, /device:TPU:6, one launch (start us, length us, event | category | flops | bytes accessed | tf_op | source)
XLA Modules:
  0.0 46.8 jit_solution(9868394292990064331)
XLA Ops:
  1.9 43.6 %shard_map.93 = (bf16[128,5120]{1,0:T(8,128)(2,1)S(1)}, bf16[128,2,640]{2,1,0:T(2,128)(2,1)S(1)}, f32[4,2,640]{2,1,0:T(2,128)S(1)}, f32[8,128]{1,0:T(8,128)S(1)}) custom-call(s32[1,1]{1,0:T(1,128)S(6)} %copy.10.refs_0_, f32[1,1]{1,0:T(1,128)S(6)} %copy.11.refs_1_, bf16[128,5120]{1,0:T(8,128)(2,1)} %bitcast.8, bf16[128,2,640]{2,1,0:T(2,128)(2,1)} %bitcast.11, ...), custom_call_target="tpu_custom_call" | custom-call | flops 1677721600 | bytes 5242880 | tf_op jit(solution)/shard_map/pallas_call | solution.py:388
  45.5 1.3 %shard_map.94 = (bf16[128,5120]{1,0:T(8,128)(2,1)}, bf16[128,2,640]{2,1,0:T(2,128)(2,1)}, f32[4,2,640]{2,1,0:T(2,128)}, f32[1,1]{1,0:T(1,128)}) custom-call(bf16[128,5120]{1,0:T(8,128)(2,1)S(1)} %get-tuple-element.12.qg, bf16[128,2,640]{2,1,0:T(2,128)(2,1)S(1)} %get-tuple-element.13.own, f32[4,2,640]{2,1,0:T(2,128)S(1)} %get-tuple-element.14.pre, ...), custom_call_target="tpu_custom_call" | custom-call | tf_op jit(solution)/shard_map/pallas_call | solution.py:448
